TPU v7x, 32 devices: a whole 2x2x4 slice. The times are simulated.
32 devices in a mesh: dp: 8 (over z, y), mp: 4 (over x, core).
Axes of the slice: x: 2, y: 2, z: 4, core: 2. Of those that a mesh axis runs over, the one named last changes fastest.
Arguments:
- tokens: bfloat16 [16384, 896], P(('dp', 'mp')), may hold values from -6 to 6
- cotangent: bfloat16 [16384, 896], P(('dp', 'mp')), may hold values from -6 to 6
- segments: int32 [8, 2048], P('dp'), may hold values from 0 to 7, never falling along the last dimension, each value on 1 to 1537 neighbouring positions
- qkv_weight: float32 [896, 1152], P('dp'), may hold values from -0.1875 to 0.1875
- qkv_moment: float32 [896, 1152], P('dp'), may hold values from -128 to 128
- qkv_square: float32 [896, 1152], P('dp'), may hold values from 32.768 to 131.072
- qkv_bias: float32 [1152], P('dp'), may hold values from -3 to 3
- bias_moment: float32 [1152], P('dp'), may hold values from -2560 to 2560
- bias_square: float32 [1152], P('dp'), may hold values from 14680.064 to 58720.258
- out_weight: float32 [896, 896], P('dp'), may hold values from -1.5 to 1.5
- out_moment: float32 [896, 896], P('dp'), may hold values from -6 to 6
- out_square: float32 [896, 896], P('dp'), may hold values from 0.24576 to 0.98304
- gate_up_weight: float32 [896, 2, 4864], P('dp', None, 'mp'), may hold values from -0.1875 to 0.1875
- gate_up_moment: float32 [896, 2, 4864], P('dp', None, 'mp'), may hold values from -40 to 40
- gate_up_square: float32 [896, 2, 4864], P('dp', None, 'mp'), may hold values from 3.2768 to 13.1072
- down_weight: float32 [4864, 896], P('mp', 'dp'), may hold values from -0.15625 to 0.15625
- down_moment: float32 [4864, 896], P('mp', 'dp'), may hold values from -48 to 48
- down_square: float32 [4864, 896], P('mp', 'dp'), may hold values from 5.89824 to 23.59296
- norm_gains: float32 [2, 896], P(None, 'dp'), may hold values from 0.5 to 1.5
- gains_moment: float32 [2, 896], P(None, 'dp'), may hold values from -128 to 128
- gains_square: float32 [2, 896], P(None, 'dp'), may hold values from 40.96 to 163.84
Outputs:
- layer_out: bfloat16 [16384, 896], P(('dp', 'mp'))
- input_grad: bfloat16 [16384, 896], P(('dp', 'mp'))
- qkv_grad: float32 [896, 1152], P('dp')
- qkv_moment_new: float32 [896, 1152], P('dp')
- qkv_square_new: float32 [896, 1152], P('dp')
- qkv_weight_new: float32 [896, 1152], P('dp')
- bias_grad: float32 [1152], P('dp')
- bias_moment_new: float32 [1152], P('dp')
- bias_square_new: float32 [1152], P('dp')
- bias_new: float32 [1152], P('dp')
- out_grad: float32 [896, 896], P('dp')
- out_moment_new: float32 [896, 896], P('dp')
- out_square_new: float32 [896, 896], P('dp')
- out_weight_new: float32 [896, 896], P('dp')
- gate_up_grad: float32 [896, 2, 4864], P('dp', None, 'mp')
- gate_up_moment_new: float32 [896, 2, 4864], P('dp', None, 'mp')
- gate_up_square_new: float32 [896, 2, 4864], P('dp', None, 'mp')
- gate_up_weight_new: float32 [896, 2, 4864], P('dp', None, 'mp')
- down_grad: float32 [4864, 896], P('mp', 'dp')
- down_moment_new: float32 [4864, 896], P('mp', 'dp')
- down_square_new: float32 [4864, 896], P('mp', 'dp')
- down_weight_new: float32 [4864, 896], P('mp', 'dp')
- gains_grad: float32 [2, 896], P(None, 'dp')
- gains_moment_new: float32 [2, 896], P(None, 'dp')
- gains_square_new: float32 [2, 896], P(None, 'dp')
- gains_new: float32 [2, 896], P(None, 'dp')
Inputs may be any that keep to these rules, and one draw needn't show every extreme that they name: `segments`: document numbers never fall along a sequence and start at 0; each document has 1 to 1537 tokens and one of each sequence has exactly 1537.
All inputs are finite; a program needn't handle non-finite values.
Results may differ from a plain program's by a relative error of at most 0.02.
Values may be sent and summed in bfloat16 or wider, within the bound.
A program may use at most 256 MiB of HBM per device.

v0:
```python
import jax
import jax.numpy as jnp
from jax import lax
from jax.sharding import PartitionSpec as P

D = 896
QUERY_HEADS = 14
KEY_VALUE_HEADS = 2
HEAD_SIZE = 64
FF = 4864
STEP = 10
QUERY_WIDTH = 896


NORM_EPS = 1e-06
ROPE_THETA = 1000000.0
BETA_FIRST = 0.9
BETA_SECOND = 0.999
ADAM_EPS = 1e-08
MASKED = -1e30


def apply_rotation(values, cosine_table, sine_lookup):
    half_dim = values.shape[-1] // 2
    first_half = values[..., :half_dim]
    second = values[..., half_dim:]
    cos_b = cosine_table[:, None, :]
    sin_b = sine_lookup[:, None, :]
    return jnp.concatenate(
        [first_half * cos_b - second * sin_b, second * cos_b + first_half * sin_b], axis=-1
    )


def rotation_backward(values, cosine_table, sine_lookup):
    half_dim = values.shape[-1] // 2
    first_half = values[..., :half_dim]
    second = values[..., half_dim:]
    cos_b = cosine_table[:, None, :]
    sin_b = sine_lookup[:, None, :]
    return jnp.concatenate(
        [first_half * cos_b + second * sin_b, second * cos_b - first_half * sin_b], axis=-1
    )


def contract_rows(left, right):
    return lax.dot_general(
        left, right, (((0,), (0,)), ((), ())), preferred_element_type=jnp.float32
    )


def contract_cols(left, right):
    return lax.dot_general(
        left, right, (((1,), (1,)), ((), ())), preferred_element_type=jnp.float32
    )


def adam_update(weight, gradient, moment, square, step_rate, decay_rate):
    new_moment = BETA_FIRST * moment + (1.0 - BETA_FIRST) * gradient
    new_square = BETA_SECOND * square + (1.0 - BETA_SECOND) * gradient * gradient
    moment_hat = new_moment / (1.0 - BETA_FIRST**STEP)
    square_hat = new_square / (1.0 - BETA_SECOND**STEP)
    updated = weight - step_rate * (
        moment_hat / (jnp.sqrt(square_hat) + ADAM_EPS) + decay_rate * weight
    )
    return (gradient, new_moment, new_square, updated)


def per_device(
    tokens,
    cotangent,
    segments,
    qkv_weight,
    qkv_moment,
    qkv_square,
    qkv_bias,
    bias_moment,
    bias_square,
    out_weight,
    out_moment,
    out_square,
    gate_up_weight,
    gate_up_moment,
    gate_up_square,
    down_weight,
    down_moment,
    down_square,
    norm_gains,
    gains_moment,
    gains_square,
):
    brain_float_cast = jnp.bfloat16
    single_precision = jnp.float32
    token_rows = tokens.shape[0]
    axis_parts = lax.axis_size("mp")
    own_index = lax.axis_index("mp")
    group_of_heads = QUERY_HEADS // KEY_VALUE_HEADS
    width_ff = down_weight.shape[0]
    score_scale = HEAD_SIZE ** (-0.5)
    w_qkv, w_out, w_gate_up, w_down = (
        lax.all_gather(qkv_weight.astype(brain_float_cast), "dp", axis=0, tiled=True),
        lax.all_gather(out_weight.astype(brain_float_cast), "dp", axis=0, tiled=True),
        lax.all_gather(gate_up_weight.astype(brain_float_cast), "dp", axis=0, tiled=True),
        lax.all_gather(down_weight.astype(brain_float_cast), "dp", axis=1, tiled=True),
    )
    bias_all, gain_all = (
        lax.all_gather(qkv_bias, "dp", axis=0, tiled=True),
        lax.all_gather(norm_gains, "dp", axis=1, tiled=True),
    )
    inputs = tokens.astype(single_precision)
    scale_one = lax.rsqrt(jnp.mean(inputs * inputs, axis=-1, keepdims=True) + NORM_EPS)
    base_one = inputs * scale_one
    normed = (base_one * gain_all[0]).astype(brain_float_cast)
    query_key_value = jnp.dot(normed, w_qkv, preferred_element_type=single_precision) + bias_all
    segrow = segments[0]
    own_seg = lax.dynamic_slice_in_dim(segrow, own_index * token_rows, token_rows)
    before = jnp.sum((segrow[None, :] < own_seg[:, None]).astype(jnp.int32), axis=1)
    query_index = own_index * token_rows + jnp.arange(token_rows, dtype=jnp.int32)
    position = query_index - before
    inverse = ROPE_THETA ** (
        -(jnp.arange(HEAD_SIZE // 2, dtype=single_precision) * 2.0) / HEAD_SIZE
    )
    angles = position.astype(single_precision)[:, None] * inverse[None, :]
    cosine_table = jnp.cos(angles)
    sine_lookup = jnp.sin(angles)
    rotated_queries = apply_rotation(
        query_key_value[:, :QUERY_WIDTH].reshape(token_rows, QUERY_HEADS, HEAD_SIZE),
        cosine_table,
        sine_lookup,
    ).astype(brain_float_cast)
    rotated_keys = apply_rotation(
        query_key_value[:, QUERY_WIDTH : QUERY_WIDTH + KEY_VALUE_HEADS * HEAD_SIZE].reshape(
            token_rows, KEY_VALUE_HEADS, HEAD_SIZE
        ),
        cosine_table,
        sine_lookup,
    )
    rotated_keys = rotated_keys.astype(brain_float_cast).reshape(
        token_rows, KEY_VALUE_HEADS * HEAD_SIZE
    )
    value_matrix = query_key_value[:, QUERY_WIDTH + KEY_VALUE_HEADS * HEAD_SIZE :].astype(
        brain_float_cast
    )
    key_all, value_all = (
        lax.all_gather(rotated_keys, "mp", axis=0, tiled=True),
        lax.all_gather(value_matrix, "mp", axis=0, tiled=True),
    )
    allowed_list = []
    for source in range(axis_parts):
        key_index = source * token_rows + jnp.arange(token_rows, dtype=jnp.int32)
        key_seg = segrow[source * token_rows : (source + 1) * token_rows]
        allowed = (key_index[None, :] <= query_index[:, None]) & (
            key_seg[None, :] == own_seg[:, None]
        )
        allowed_list.append(jnp.repeat(allowed, group_of_heads, axis=0))

    def block_scores(q_block, key_value_head, source):
        key_block = key_all[
            source * token_rows : (source + 1) * token_rows,
            key_value_head * HEAD_SIZE : (key_value_head + 1) * HEAD_SIZE,
        ]
        raw_scores = contract_cols(q_block, key_block) * score_scale
        return jnp.where(allowed_list[source], raw_scores, MASKED)

    query_list = []
    log_totals = []
    head_outputs = []
    for key_value_head in range(KEY_VALUE_HEADS):
        q_block = rotated_queries[
            :, key_value_head * group_of_heads : (key_value_head + 1) * group_of_heads, :
        ].reshape(token_rows * group_of_heads, HEAD_SIZE)
        query_list.append(q_block)
        row_top = jnp.full((token_rows * group_of_heads,), MASKED, single_precision)
        row_total = jnp.zeros((token_rows * group_of_heads,), single_precision)
        for source in range(axis_parts):
            scores = block_scores(q_block, key_value_head, source)
            new_top = jnp.maximum(row_top, jnp.max(scores, axis=-1))
            shifted = jnp.where(allowed_list[source], jnp.exp(scores - new_top[:, None]), 0.0)
            row_total = row_total * jnp.exp(row_top - new_top) + jnp.sum(shifted, axis=-1)
            row_top = new_top
        log_total = row_top + jnp.log(row_total)
        log_totals.append(log_total)
        attended_part = jnp.zeros((token_rows * group_of_heads, HEAD_SIZE), single_precision)
        for source in range(axis_parts):
            scores = block_scores(q_block, key_value_head, source)
            prob_block = jnp.where(
                allowed_list[source], jnp.exp(scores - log_total[:, None]), 0.0
            ).astype(brain_float_cast)
            value_block = value_all[
                source * token_rows : (source + 1) * token_rows,
                key_value_head * HEAD_SIZE : (key_value_head + 1) * HEAD_SIZE,
            ]
            attended_part = attended_part + jnp.dot(
                prob_block, value_block, preferred_element_type=single_precision
            )
        head_outputs.append(attended_part.reshape(token_rows, group_of_heads, HEAD_SIZE))
    attention_output = jnp.stack(head_outputs, axis=1).reshape(token_rows, QUERY_WIDTH)
    attended_low = attention_output.astype(brain_float_cast)
    hidden = inputs + jnp.dot(attended_low, w_out, preferred_element_type=single_precision)
    scale_two = lax.rsqrt(jnp.mean(hidden * hidden, axis=-1, keepdims=True) + NORM_EPS)
    base_two = hidden * scale_two
    normed_two = (base_two * gain_all[1]).astype(brain_float_cast)
    normed_all = lax.all_gather(normed_two, "mp", axis=0, tiled=True)
    joined = w_gate_up.reshape(D, 2 * width_ff)
    gate_up = jnp.dot(normed_all, joined, preferred_element_type=single_precision)
    gate_pre = gate_up[:, :width_ff]
    up_pre = gate_up[:, width_ff:]
    sig_gate = jax.nn.sigmoid(gate_pre)
    silu_gate = gate_pre * sig_gate
    active = (silu_gate * up_pre).astype(brain_float_cast)
    mlp_sum = lax.psum_scatter(
        jnp.dot(active, w_down, preferred_element_type=single_precision).astype(jnp.bfloat16),
        "mp",
        scatter_dimension=0,
        tiled=True,
    ).astype(jnp.float32)
    layer_out = (hidden + mlp_sum).astype(brain_float_cast)
    grad_out = cotangent.astype(single_precision)
    back_all = lax.all_gather(cotangent, "mp", axis=0, tiled=True)
    grad_active = contract_cols(back_all, w_down)
    grad_down = contract_rows(active, back_all)
    grad_gate = (grad_active * up_pre * sig_gate * (1.0 + gate_pre * (1.0 - sig_gate))).astype(
        brain_float_cast
    )
    grad_up = (grad_active * silu_gate).astype(brain_float_cast)
    grad_both = jnp.concatenate([grad_gate, grad_up], axis=1)
    grad_gate_up = contract_rows(normed_all, grad_both).reshape(D, 2, width_ff)
    grad_normed_two = lax.psum_scatter(
        contract_cols(grad_both, joined).astype(jnp.bfloat16), "mp", scatter_dimension=0, tiled=True
    ).astype(jnp.float32)
    grad_gain_two = jnp.sum(grad_normed_two * base_two, axis=0)
    scaled_two = grad_normed_two * gain_all[1]
    grad_hidden = grad_out + scale_two * (
        scaled_two - base_two * jnp.mean(scaled_two * base_two, axis=-1, keepdims=True)
    )
    grad_branch = grad_hidden.astype(brain_float_cast)
    grad_out_w = contract_rows(attended_low, grad_branch)
    attention_output_grad = contract_cols(grad_branch, w_out).astype(brain_float_cast)
    heads_gradient = attention_output_grad.reshape(
        token_rows, KEY_VALUE_HEADS, group_of_heads, HEAD_SIZE
    )
    correction = jnp.sum(
        heads_gradient.astype(single_precision)
        * attention_output.reshape(token_rows, KEY_VALUE_HEADS, group_of_heads, HEAD_SIZE),
        axis=-1,
    )
    grad_query_heads = []
    grad_key_heads = []
    grad_value_heads = []
    for key_value_head in range(KEY_VALUE_HEADS):
        q_block = query_list[key_value_head]
        log_total = log_totals[key_value_head]
        grad_rows_head = heads_gradient[:, key_value_head].reshape(
            token_rows * group_of_heads, HEAD_SIZE
        )
        row_delta = correction[:, key_value_head].reshape(token_rows * group_of_heads)
        grad_query = jnp.zeros((token_rows * group_of_heads, HEAD_SIZE), single_precision)
        key_parts = []
        value_parts = []
        for source in range(axis_parts):
            scores = block_scores(q_block, key_value_head, source)
            prob_block = jnp.where(allowed_list[source], jnp.exp(scores - log_total[:, None]), 0.0)
            key_block = key_all[
                source * token_rows : (source + 1) * token_rows,
                key_value_head * HEAD_SIZE : (key_value_head + 1) * HEAD_SIZE,
            ]
            value_block = value_all[
                source * token_rows : (source + 1) * token_rows,
                key_value_head * HEAD_SIZE : (key_value_head + 1) * HEAD_SIZE,
            ]
            grad_prob = contract_cols(grad_rows_head, value_block)
            grad_score = (prob_block * (grad_prob - row_delta[:, None])).astype(brain_float_cast)
            grad_query = (
                grad_query
                + jnp.dot(grad_score, key_block, preferred_element_type=single_precision)
                * score_scale
            )
            key_parts.append(contract_rows(grad_score, q_block) * score_scale)
            value_parts.append(contract_rows(prob_block.astype(brain_float_cast), grad_rows_head))
        grad_query_heads.append(grad_query.reshape(token_rows, group_of_heads, HEAD_SIZE))
        grad_key_heads.append(jnp.concatenate(key_parts, axis=0))
        grad_value_heads.append(jnp.concatenate(value_parts, axis=0))
    grad_key_all = jnp.concatenate(grad_key_heads, axis=1)
    grad_value_all = jnp.concatenate(grad_value_heads, axis=1)
    key_gradient, grad_value = (
        lax.psum_scatter(
            grad_key_all.astype(jnp.bfloat16), "mp", scatter_dimension=0, tiled=True
        ).astype(jnp.float32),
        lax.psum_scatter(
            grad_value_all.astype(jnp.bfloat16), "mp", scatter_dimension=0, tiled=True
        ).astype(jnp.float32),
    )
    grad_query_all = jnp.stack(grad_query_heads, axis=1).reshape(token_rows, QUERY_HEADS, HEAD_SIZE)
    grad_query_all = rotation_backward(grad_query_all, cosine_table, sine_lookup).reshape(
        token_rows, QUERY_WIDTH
    )
    key_gradient = rotation_backward(
        key_gradient.reshape(token_rows, KEY_VALUE_HEADS, HEAD_SIZE), cosine_table, sine_lookup
    ).reshape(token_rows, KEY_VALUE_HEADS * HEAD_SIZE)
    grad_qkv = jnp.concatenate([grad_query_all, key_gradient, grad_value], axis=1).astype(
        brain_float_cast
    )
    grad_bias = jnp.sum(grad_qkv.astype(single_precision), axis=0)
    grad_qkv_w = contract_rows(normed, grad_qkv)
    grad_normed = contract_cols(grad_qkv, w_qkv)
    grad_gain_one = jnp.sum(grad_normed * base_one, axis=0)
    scaled_one = grad_normed * gain_all[0]
    grad_inputs = grad_hidden + scale_one * (
        scaled_one - base_one * jnp.mean(scaled_one * base_one, axis=-1, keepdims=True)
    )
    input_grad = grad_inputs.astype(brain_float_cast)
    grad_gains = jnp.stack([grad_gain_one, grad_gain_two], axis=0)
    grad_qkv_w, grad_out_w, grad_bias, grad_gains = (
        lax.psum(grad_qkv_w.astype(jnp.bfloat16), "mp").astype(jnp.float32),
        lax.psum(grad_out_w.astype(jnp.bfloat16), "mp").astype(jnp.float32),
        lax.psum(grad_bias.astype(jnp.bfloat16), "mp").astype(jnp.float32),
        lax.psum(grad_gains.astype(jnp.bfloat16), "mp").astype(jnp.float32),
    )
    owned_qkv, owned_out, owned_bias, owned_gains, owned_gate_up, owned_down = (
        lax.psum_scatter(grad_qkv_w, "dp", scatter_dimension=0, tiled=True),
        lax.psum_scatter(grad_out_w, "dp", scatter_dimension=0, tiled=True),
        lax.psum_scatter(grad_bias, "dp", scatter_dimension=0, tiled=True),
        lax.psum_scatter(grad_gains, "dp", scatter_dimension=1, tiled=True),
        lax.psum_scatter(grad_gate_up, "dp", scatter_dimension=0, tiled=True),
        lax.psum_scatter(grad_down, "dp", scatter_dimension=1, tiled=True),
    )
    upd_qkv = adam_update(qkv_weight, owned_qkv, qkv_moment, qkv_square, 1.5 * D ** (-0.5), 0.1)
    upd_bias = adam_update(qkv_bias, owned_bias, bias_moment, bias_square, 0.3, 0.0)
    upd_out = adam_update(
        out_weight,
        owned_out,
        out_moment,
        out_square,
        1.5 * max(4, QUERY_WIDTH // 64) ** (-0.5),
        0.1,
    )
    upd_gate_up = adam_update(
        gate_up_weight, owned_gate_up, gate_up_moment, gate_up_square, 1.5 * D ** (-0.5), 0.1
    )
    upd_down = adam_update(
        down_weight, owned_down, down_moment, down_square, 1.5 * (FF // 3) ** (-0.5), 0.1
    )
    upd_gains = adam_update(norm_gains, owned_gains, gains_moment, gains_square, 0.6, 0.0)
    return (
        layer_out,
        input_grad,
        upd_qkv[0],
        upd_qkv[1],
        upd_qkv[2],
        upd_qkv[3],
        upd_bias[0],
        upd_bias[1],
        upd_bias[2],
        upd_bias[3],
        upd_out[0],
        upd_out[1],
        upd_out[2],
        upd_out[3],
        upd_gate_up[0],
        upd_gate_up[1],
        upd_gate_up[2],
        upd_gate_up[3],
        upd_down[0],
        upd_down[1],
        upd_down[2],
        upd_down[3],
        upd_gains[0],
        upd_gains[1],
        upd_gains[2],
        upd_gains[3],
    )


def solution(mesh):
    placed = (
        P(("dp", "mp"), None),
        P(("dp", "mp"), None),
        P("dp", None),
        P("dp", None),
        P("dp", None),
        P("dp", None),
        P("dp"),
        P("dp"),
        P("dp"),
        P("dp", None),
        P("dp", None),
        P("dp", None),
        P("dp", None, "mp"),
        P("dp", None, "mp"),
        P("dp", None, "mp"),
        P("mp", "dp"),
        P("mp", "dp"),
        P("mp", "dp"),
        P(None, "dp"),
        P(None, "dp"),
        P(None, "dp"),
    )
    return jax.shard_map(
        per_device,
        mesh=mesh,
        in_specs=placed,
        out_specs=(
            P(("dp", "mp"), None),
            P(("dp", "mp"), None),
            P("dp", None),
            P("dp", None),
            P("dp", None),
            P("dp", None),
            P("dp"),
            P("dp"),
            P("dp"),
            P("dp"),
            P("dp", None),
            P("dp", None),
            P("dp", None),
            P("dp", None),
            P("dp", None, "mp"),
            P("dp", None, "mp"),
            P("dp", None, "mp"),
            P("dp", None, "mp"),
            P("mp", "dp"),
            P("mp", "dp"),
            P("mp", "dp"),
            P("mp", "dp"),
            P(None, "dp"),
            P(None, "dp"),
            P(None, "dp"),
            P(None, "dp"),
        ),
        check_vma=False,
    )
```

profile of v0, /device:TPU:0, one launch (start us, length us, event | category | flops | bytes accessed | tf_op | source)
XLA Modules:
  0.0 1343.2 jit_solution(17910815964922238396)
XLA Ops:
  14.7 22.3 %all-gather = f32[8,112,2]{1,2,0:T(2,128)S(1)} all-gather(f32[1,112,2]{1,2,0:T(2,128)S(1)} %bitcast.156), channel_id=1, replica_groups=mesh['dp'=8,'mp'=4] {'dp'}, dimensions={0}, use_global_device_ids=true | all-gather | bytes 8064 | tf_op jit(solution)/shard_map/all_gather | solution.py:107
  39.0 18.6 %all-reduce = f32[1152]{0:T(1024)} all-reduce(f32[1152]{0:T(1024)S(1)} %dynamic-update-slice), channel_id=1, replica_groups=mesh['dp'=8,'mp'=4] {'dp'}, use_global_device_ids=true, to_apply=%add | all-reduce | flops 1152 | bytes 9216
  76.8 11.9 reshape.341
  234.6 13.7 %copy.317 = bf16[896,2,1216]{0,2,1:T(8,128)(2,1)} copy(bf16[896,2,1216]{2,1,0:T(2,128)(2,1)} %all-gather.14.cloned.1.call-done) | data formatting | bytes 8716288 | tf_op jit(solution)/shard_map/all_gather | solution.py:102
  248.3 13.5 %all-gather.12.cloned.1.call-done = bf16[2048,896]{1,0:T(8,128)(2,1)} async-done(((bf16[512,896]{1,0:T(8,128)(2,1)}), bf16[2048,896]{1,0:T(8,128)(2,1)}) %all-gather.12.cloned.1.call-update) | async-done | bytes 3670032 | tf_op jit(solution)/shard_map/all_gather | solution.py:202
  261.8 17.6 %fusion.135 = f32[2048,2432]{1,0:T(8,128)} fusion(bf16[2048,896]{1,0:T(8,128)(2,1)} %all-gather.12.cloned.1.call-done, bf16[896,2432]{0,1:T(8,128)(2,1)} %bitcast.133), kind=kOutput, calls=%fused_computation.252 | convolution fusion | flops 8925478912 | bytes 27951104 | tf_op jit(solution)/shard_map/dot_general | solution.py:204
  279.4 36.4 %all-gather.16.cloned.1.call-done = bf16[1216,896]{0,1:T(8,128)(2,1)} async-done(((bf16[1216,112]{0,1:T(8,128)(2,1)}), bf16[1216,896]{0,1:T(8,128)(2,1)}) %all-gather.16.cloned.1.call-update) | async-done | bytes 2179088 | tf_op jit(solution)/shard_map/all_gather | solution.py:103
  315.8 31.5 %all-gather.18.cloned.1.call-done = bf16[2048,896]{1,0:T(8,128)(2,1)} async-done(((bf16[512,896]{1,0:T(8,128)(2,1)}), bf16[2048,896]{1,0:T(8,128)(2,1)}) %all-gather.18.cloned.1.call-update) | async-done | bytes 3670032 | tf_op jit(solution)/shard_map/all_gather | solution.py:218
  347.3 17.6 %multiply_convert_fusion.1 = (bf16[2048,1216]{1,0:T(8,128)(2,1)}, bf16[2048,1216]{1,0:T(8,128)(2,1)}, bf16[2048,1216]{1,0:T(8,128)(2,1)}) fusion(f32[2048,2432]{1,0:T(8,128)} %fusion.135, bf16[2048,896]{1,0:T(8,128)(2,1)} %all-gather.18.cloned.1.call-done, bf16[1216,896]{0,1:T(8,128)(2,1)} %all-gather.16.cloned.1.call-done), kind=kOutput, calls=%fused_computation.1 | convolution fusion | flops 4500094976 | bytes 40714240 | tf_op jit(solution)/shard_map/dot_general | solution.py:52
  364.8 16.2 %fusion.13 = bf16[2048,896]{1,0:T(8,128)(2,1)} fusion(bf16[896,2432]{0,1:T(8,128)(2,1)} %bitcast.134, bf16[2048,1216]{1,0:T(8,128)(2,1)} %get-tuple-element.122, bf16[2048,1216]{1,0:T(8,128)(2,1)} %get-tuple-element.121), kind=kOutput, calls=%fused_computation.63 | convolution fusion | flops 8947236864 | bytes 17989632 | tf_op jit(solution)/shard_map/dot_general | solution.py:52
  381.1 9.7 convolution_convert_fusion.1
  390.9 31.6 %reduce-scatter.13.cloned.1.call-done = bf16[512,896]{1,0:T(8,128)(2,1)} async-done(((bf16[2048,896]{1,0:T(8,128)(2,1)}), bf16[512,896]{1,0:T(8,128)(2,1)}) %reduce-scatter.13.cloned.1.call-update) | async-done | bytes 917520 | tf_op jit(solution)/shard_map/reduce_scatter | solution.py:227
  424.3 42.1 %reduce-scatter.11.cloned.1.call-done = bf16[512,896]{1,0:T(8,128)(2,1)} async-done(((bf16[2048,896]{1,0:T(8,128)(2,1)}), bf16[512,896]{1,0:T(8,128)(2,1)}) %reduce-scatter.11.cloned.1.call-update) | async-done | bytes 917520 | tf_op jit(solution)/shard_map/reduce_scatter | solution.py:210
  605.8 17.7 %reduce-scatter.17.cloned.1.call-done = bf16[512,128]{0,1:T(8,128)(2,1)} async-done(((bf16[2048,128]{0,1:T(8,128)(2,1)}), bf16[512,128]{0,1:T(8,128)(2,1)}) %reduce-scatter.17.cloned.1.call-update) | async-done | bytes 131088 | tf_op jit(solution)/shard_map/reduce_scatter | solution.py:288
  641.0 23.6 %fusion.1 = f32[896,2432]{0,1:T(8,128)} fusion(bf16[2048,896]{1,0:T(8,128)(2,1)} %all-gather.12.cloned.1.call-done, bf16[2048,1216]{1,0:T(8,128)(2,1)} %get-tuple-element.122, bf16[2048,1216]{1,0:T(8,128)(2,1)} %get-tuple-element.121), kind=kOutput, calls=%fused_computation.38 | convolution fusion | flops 8945401856 | bytes 22347776 | tf_op jit(solution)/shard_map/dot_general | solution.py:46
  664.6 15.9 %copy.338 = f32[896,2,1216]{2,1,0:T(2,128)} copy(f32[896,2,1216]{0,2,1:T(8,128)} %bitcast.128) | data formatting | bytes 17432576 | tf_op jit(solution)/shard_map/reshape | solution.py:226
  680.8 10.7 fusion.136
  691.6 13.5 %all-reduce.10.cloned.1.call-done = (bf16[896,1152]{1,0:T(8,128)(2,1)}, bf16[896,896]{1,0:T(8,128)(2,1)}) async-done(((bf16[896,1152]{1,0:T(8,128)(2,1)}, bf16[896,896]{1,0:T(8,128)(2,1)}), (bf16[896,1152]{1,0:T(8,128)(2,1)}, bf16[896,896]{1,0:T(8,128)(2,1)})) %all-reduce.10.cloned.1.call-update) | async-done | bytes 3670032 | tf_op jit(solution)/shard_map/psum | solution.py:313
  713.8 21.7 %all-reduce.1 = f32[1152]{0:T(1024)S(1)} all-reduce(bf16[1152]{0:T(1024)(128)(2,1)S(1)} %get-tuple-element.92), channel_id=7, replica_groups=mesh['dp'=8,'mp'=4] {'dp'}, use_global_device_ids=true, to_apply=%region_30.31.clone | all-reduce | flops 1152 | bytes 6912
  739.6 31.3 %reduce-scatter.25.cloned.1.call-done = f32[112,2]{1,0:T(8,128)} async-done(((f32[896,2]{1,0:T(8,128)}), f32[112,2]{1,0:T(8,128)}) %reduce-scatter.25.cloned.1.call-update) | async-done | bytes 912
  772.4 293.8 %all-reduce.8.cloned.1.call-done = f32[896,2,1216]{2,1,0:T(2,128)} async-done(((f32[896,2,1216]{2,1,0:T(2,128)}), f32[896,2,1216]{2,1,0:T(2,128)}) %all-reduce.8.cloned.1.call-update) | async-done | bytes 8716304
  1076.2 87.1 %reduce-scatter.23.cloned.1.call-done = f32[1216,112]{0,1:T(8,128)} async-done(((f32[1216,896]{0,1:T(8,128)}), f32[1216,112]{0,1:T(8,128)}) %reduce-scatter.23.cloned.1.call-update) | async-done | bytes 544784 | tf_op jit(solution)/shard_map/reduce_scatter | solution.py:324
  1165.8 77.5 %reduce-scatter.21.cloned.1.call-done = f32[112,896]{1,0:T(8,128)} async-done(((f32[896,896]{1,0:T(8,128)}), f32[112,896]{1,0:T(8,128)}) %reduce-scatter.21.cloned.1.call-update) | async-done | bytes 401424 | tf_op jit(solution)/shard_map/reduce_scatter | solution.py:320
  1245.7 88.2 %reduce-scatter.19.cloned.1.call-done = f32[112,1152]{1,0:T(8,128)} async-done(((f32[896,1152]{1,0:T(8,128)}), f32[112,1152]{1,0:T(8,128)}) %reduce-scatter.19.cloned.1.call-update) | async-done | bytes 516112 | tf_op jit(solution)/shard_map/reduce_scatter | solution.py:319
  (465 shorter events, 361.5 us)
Async XLA Ops:
  7.3 93.5 %all-gather.8.cloned.1.call-start = ((), (), s32[]{:S(2)}) async-start(), calls=%async_computation.8 | async-start | bytes 2322432 | tf_op jit(solution)/shard_map/all_gather | solution.py:100
  9.2 218.4 %all-gather.10.cloned.1.call-start = ((), (), s32[]{:S(2)}) async-start(), calls=%async_computation.9 | async-start | bytes 1806336 | tf_op jit(solution)/shard_map/all_gather | solution.py:101
  10.9 223.7 %all-gather.14.cloned.1.call-start = ((), (), s32[]{:S(2)}) async-start(), calls=%async_computation.11 | async-start | bytes 5160960 | tf_op jit(solution)/shard_map/all_gather | solution.py:102
  13.5 248.3 %all-gather.12.cloned.1.call-start = ((), (), s32[]{:S(2)}) async-start(), calls=%async_computation.10 | async-start | bytes 4587520 | tf_op jit(solution)/shard_map/all_gather | solution.py:202
  232.1 83.7 %all-gather.16.cloned.1.call-start = ((), (), s32[]{:S(2)}) async-start(), calls=%async_computation.12 | async-start | bytes 2580480 | tf_op jit(solution)/shard_map/all_gather | solution.py:103
  234.0 113.3 %all-gather.18.cloned.1.call-start = ((), (), s32[]{:S(2)}) async-start(), calls=%async_computation.14 | async-start | bytes 4587520 | tf_op jit(solution)/shard_map/all_gather | solution.py:218
  234.6 187.9 %reduce-scatter.13.cloned.1.call-start = ((), (), s32[]{:S(2)}) async-start(), calls=%async_computation.15 | async-start | bytes 4587520 | tf_op jit(solution)/shard_map/reduce_scatter | solution.py:227
  381.1 85.4 %reduce-scatter.11.cloned.1.call-start = ((), (), s32[]{:S(2)}) async-start(), calls=%async_computation.13 | async-start | bytes 4587520 | tf_op jit(solution)/shard_map/reduce_scatter | solution.py:210
  390.8 214.0 %reduce-scatter.15.cloned.1.call-start = ((), (), s32[]{:S(2)}) async-start(), calls=%async_computation.16 | async-start | bytes 655360 | tf_op jit(solution)/shard_map/reduce_scatter | solution.py:285
  576.8 46.6 %reduce-scatter.17.cloned.1.call-start = ((), (), s32[]{:S(2)}) async-start(), calls=%async_computation.17 | async-start | bytes 655360 | tf_op jit(solution)/shard_map/reduce_scatter | solution.py:288
  598.9 106.3 %all-reduce.10.cloned.1.call-start = ((), (), s32[]{:S(2)}) async-start(), calls=%async_computation.23 | async-start | bytes 7340032 | tf_op jit(solution)/shard_map/psum | solution.py:313
  627.6 143.3 %reduce-scatter.25.cloned.1.call-start = ((), (), s32[]{:S(2)}) async-start(), calls=%async_computation.21 | async-start | bytes 516096
  641.0 425.2 %all-reduce.8.cloned.1.call-start = ((), (), s32[]{:S(2)}) async-start(), calls=%async_computation.22 | async-start | bytes 18350080
  680.6 482.7 %reduce-scatter.23.cloned.1.call-start = ((), (), s32[]{:S(2)}) async-start(), calls=%async_computation.20 | async-start | bytes 5160960 | tf_op jit(solution)/shard_map/reduce_scatter | solution.py:324
  691.6 551.7 %reduce-scatter.21.cloned.1.call-start = ((), (), s32[]{:S(2)}) async-start(), calls=%async_computation.19 | async-start | bytes 3612672 | tf_op jit(solution)/shard_map/reduce_scatter | solution.py:320
  708.5 625.4 %reduce-scatter.19.cloned.1.call-start = ((), (), s32[]{:S(2)}) async-start(), calls=%async_computation.18 | async-start | bytes 4644864 | tf_op jit(solution)/shard_map/reduce_scatter | solution.py:319
  736.2 331.3 %copy-start.56 = (f32[112,2,1216]{2,1,0:T(2,128)S(1)}, f32[112,2,1216]{2,1,0:T(2,128)}, u32[]{:S(2)}) copy-start(f32[112,2,1216]{2,1,0:T(2,128)} %param.33) | copy-start | bytes 3268612
  771.8 298.7 %copy-start.84 = (f32[2,112]{1,0:T(2,128)}, f32[2,112]{1,0:T(2,128)S(1)}, u32[]{:S(2)}) copy-start(f32[2,112]{1,0:T(2,128)S(1)} %copy.360) | copy-start | bytes 2692
  1070.5 92.8 %copy-start.60 = (f32[1216,112]{0,1:T(8,128)S(1)}, f32[1216,112]{0,1:T(8,128)}, u32[]{:S(2)}) copy-start(f32[1216,112]{0,1:T(8,128)} %param.36) | copy-start | bytes 1634308
  1070.5 92.8 %copy-start.70 = (f32[1216,112]{0,1:T(8,128)S(1)}, f32[1216,112]{0,1:T(8,128)}, u32[]{:S(2)}) copy-start(f32[1216,112]{0,1:T(8,128)} %param.38) | copy-start | bytes 1634308
  1070.5 92.7 %copy-start.71 = (f32[1216,112]{0,1:T(8,128)S(1)}, f32[1216,112]{0,1:T(8,128)}, u32[]{:S(2)}) copy-start(f32[1216,112]{0,1:T(8,128)} %param.37) | copy-start | bytes 1634308
  1074.3 169.0 %copy-start.68 = (f32[112,896]{1,0:T(8,128)S(1)}, f32[112,896]{1,0:T(8,128)}, u32[]{:S(2)}) copy-start(f32[112,896]{1,0:T(8,128)} %param.30) | copy-start | bytes 1204228
  1076.2 257.7 %copy-start.62 = (f32[112,1152]{1,0:T(8,128)S(1)}, f32[112,1152]{1,0:T(8,128)}, u32[]{:S(2)}) copy-start(f32[112,1152]{1,0:T(8,128)} %param.24) | copy-start | bytes 1548292
  1076.2 257.7 %copy-start.72 = (f32[112,1152]{1,0:T(8,128)S(1)}, f32[112,1152]{1,0:T(8,128)}, u32[]{:S(2)}) copy-start(f32[112,1152]{1,0:T(8,128)} %param.26) | copy-start | bytes 1548292
  (116 other events, 1363.5 us)
Sparse Core Ops, SparseCore 0:
  10.8 52.1 all-gather.7
  65.8 43.3 all-gather.9
  111.9 77.2 all-gather.13
  232.2 29.5 all-gather.11
  264.4 51.3 all-gather.15
  317.2 30.0 all-gather.17
  381.2 41.2 reduce-scatter.12
  425.2 41.2 reduce-scatter.10
  576.9 21.6 reduce-scatter.14
  601.7 21.6 reduce-scatter.16
  627.7 77.3 all-reduce.9
  708.9 61.9 reduce-scatter.24
  775.3 290.8 all-reduce.7
  1070.7 92.5 reduce-scatter.22
  1167.7 75.5 reduce-scatter.20
  1247.3 86.6 reduce-scatter.18
where the time goes:
time: 1350 us; the launch traced here: 1340 us
  waiting for transfers between devices  765 us (57%)
  matrix products  256 us (19%)
  local copies, waits for them, and re-layouts  144 us (11%)
  blocking collectives  83.4 us (6%)
  other arithmetic  75.8 us (6%)
  between operations  18 us (1%)
    unnamed x18, waiting for transfers between devices  326 us
    dot_general x20, matrix products, contract_cols(): lax.dot_general(left, right, (((1,), (1,)), ((), ())), preferred_element_...  109 us
    reduce_scatter x1, waiting for transfers between devices, per_device(): lax.psum_scatter(grad_qkv_w, 'dp', scatter_dimension=0, tiled=True)  88.2 us
    reduce_scatter x1, waiting for transfers between devices, per_device(): lax.psum_scatter(grad_down, 'dp', scatter_dimension=1, tiled=True)  87.1 us
    dot_general x20, matrix products, contract_rows(): lax.dot_general(left, right, (((0,), (0,)), ((), ())), preferred_element_...  79.2 us
    reduce_scatter x1, waiting for transfers between devices, per_device(): lax.psum_scatter(grad_out_w, 'dp', scatter_dimension=0, tiled=True)  77.5 us
    reduce_scatter x1, waiting for transfers between devices, per_device(): lax.psum_scatter(jnp.dot(active, w_down, preferred_element_type=single_pr...  42.1 us
    unnamed x2, blocking collectives  40.3 us
  transfers between devices with their start and end apart: 16, of which 12 were waited for; matrix products, arithmetic and copies ran while one was open for 24% of the time, Pallas kernels for 0%

commit v1 on v0

--- a/solution.py
+++ b/solution.py
@@ -10,6 +10,7 @@
 FF = 4864
 STEP = 10
 QUERY_WIDTH = 896
+QKV = 1152
 
 
 NORM_EPS = 1e-06
@@ -96,16 +97,39 @@
     group_of_heads = QUERY_HEADS // KEY_VALUE_HEADS
     width_ff = down_weight.shape[0]
     score_scale = HEAD_SIZE ** (-0.5)
-    w_qkv, w_out, w_gate_up, w_down = (
-        lax.all_gather(qkv_weight.astype(brain_float_cast), "dp", axis=0, tiled=True),
-        lax.all_gather(out_weight.astype(brain_float_cast), "dp", axis=0, tiled=True),
-        lax.all_gather(gate_up_weight.astype(brain_float_cast), "dp", axis=0, tiled=True),
-        lax.all_gather(down_weight.astype(brain_float_cast), "dp", axis=1, tiled=True),
-    )
-    bias_all, gain_all = (
-        lax.all_gather(qkv_bias, "dp", axis=0, tiled=True),
-        lax.all_gather(norm_gains, "dp", axis=1, tiled=True),
-    )
+    owned_width = qkv_bias.shape[0]
+    gain_width = norm_gains.shape[1]
+    owned_rows = qkv_weight.shape[0]
+    vectors = jnp.concatenate([qkv_bias, norm_gains[0], norm_gains[1]])
+    vectors_high = vectors.astype(brain_float_cast)
+    vectors_low = (vectors - vectors_high.astype(single_precision)).astype(brain_float_cast)
+    packed = jnp.concatenate([vectors_high, vectors_low])
+    packed = jnp.pad(packed, (0, owned_rows * 128 - packed.shape[0])).reshape(owned_rows, 128)
+    first_gather = lax.all_gather(
+        jnp.concatenate([qkv_weight.astype(brain_float_cast), packed], axis=1),
+        "dp",
+        axis=0,
+        tiled=True,
+    )
+    w_qkv = first_gather[:, :QKV]
+    used = vectors.shape[0]
+    unpacked = first_gather[:, QKV:].reshape(-1, owned_rows * 128).astype(single_precision)
+    unpacked = unpacked[:, :used] + unpacked[:, used : 2 * used]
+    bias_all = unpacked[:, :owned_width].reshape(-1)
+    gain_all = (
+        unpacked[:, owned_width : owned_width + gain_width].reshape(-1),
+        unpacked[:, owned_width + gain_width :].reshape(-1),
+    )
+    w_out = lax.all_gather(out_weight.astype(brain_float_cast), "dp", axis=0, tiled=True)
+    w_ffn = lax.all_gather(
+        jnp.concatenate([gate_up_weight[:, 0], gate_up_weight[:, 1], down_weight.T], axis=1).astype(
+            brain_float_cast
+        ),
+        "dp",
+        axis=0,
+        tiled=True,
+    )
+    back_all = lax.all_gather(cotangent, "mp", axis=0, tiled=True)
     inputs = tokens.astype(single_precision)
     scale_one = lax.rsqrt(jnp.mean(inputs * inputs, axis=-1, keepdims=True) + NORM_EPS)
     base_one = inputs * scale_one
@@ -140,10 +164,11 @@
     value_matrix = query_key_value[:, QUERY_WIDTH + KEY_VALUE_HEADS * HEAD_SIZE :].astype(
         brain_float_cast
     )
-    key_all, value_all = (
-        lax.all_gather(rotated_keys, "mp", axis=0, tiled=True),
-        lax.all_gather(value_matrix, "mp", axis=0, tiled=True),
-    )
+    key_value_all = lax.all_gather(
+        jnp.concatenate([rotated_keys, value_matrix], axis=1), "mp", axis=0, tiled=True
+    )
+    key_all = key_value_all[:, : KEY_VALUE_HEADS * HEAD_SIZE]
+    value_all = key_value_all[:, KEY_VALUE_HEADS * HEAD_SIZE :]
     allowed_list = []
     for source in range(axis_parts):
         key_index = source * token_rows + jnp.arange(token_rows, dtype=jnp.int32)
@@ -200,33 +225,46 @@
     base_two = hidden * scale_two
     normed_two = (base_two * gain_all[1]).astype(brain_float_cast)
     normed_all = lax.all_gather(normed_two, "mp", axis=0, tiled=True)
-    joined = w_gate_up.reshape(D, 2 * width_ff)
+    joined = w_ffn[:, : 2 * width_ff]
+    w_down_t = w_ffn[:, 2 * width_ff :]
     gate_up = jnp.dot(normed_all, joined, preferred_element_type=single_precision)
     gate_pre = gate_up[:, :width_ff]
     up_pre = gate_up[:, width_ff:]
     sig_gate = jax.nn.sigmoid(gate_pre)
     silu_gate = gate_pre * sig_gate
     active = (silu_gate * up_pre).astype(brain_float_cast)
+    grad_out = cotangent.astype(single_precision)
+    grad_active = jnp.dot(back_all, w_down_t, preferred_element_type=single_precision)
+    grad_gate = (grad_active * up_pre * sig_gate * (1.0 + gate_pre * (1.0 - sig_gate))).astype(
+        brain_float_cast
+    )
+    grad_up = (grad_active * silu_gate).astype(brain_float_cast)
+    grad_both = jnp.concatenate([grad_gate, grad_up], axis=1)
+    normed_partial = contract_cols(grad_both, joined).astype(brain_float_cast)
+    grad_normed_two = lax.psum_scatter(
+        normed_partial, "mp", scatter_dimension=0, tiled=True
+    ).astype(jnp.float32)
+    active, grad_both, normed_partial = lax.optimization_barrier(
+        (active, grad_both, normed_partial)
+    )
     mlp_sum = lax.psum_scatter(
-        jnp.dot(active, w_down, preferred_element_type=single_precision).astype(jnp.bfloat16),
+        contract_cols(active, w_down_t).astype(jnp.bfloat16),
         "mp",
         scatter_dimension=0,
         tiled=True,
     ).astype(jnp.float32)
     layer_out = (hidden + mlp_sum).astype(brain_float_cast)
-    grad_out = cotangent.astype(single_precision)
-    back_all = lax.all_gather(cotangent, "mp", axis=0, tiled=True)
-    grad_active = contract_cols(back_all, w_down)
-    grad_down = contract_rows(active, back_all)
-    grad_gate = (grad_active * up_pre * sig_gate * (1.0 + gate_pre * (1.0 - sig_gate))).astype(
-        brain_float_cast
-    )
-    grad_up = (grad_active * silu_gate).astype(brain_float_cast)
-    grad_both = jnp.concatenate([grad_gate, grad_up], axis=1)
-    grad_gate_up = contract_rows(normed_all, grad_both).reshape(D, 2, width_ff)
-    grad_normed_two = lax.psum_scatter(
-        contract_cols(grad_both, joined).astype(jnp.bfloat16), "mp", scatter_dimension=0, tiled=True
-    ).astype(jnp.float32)
+    grad_ffn = jnp.concatenate(
+        [
+            contract_rows(normed_all, grad_both).astype(brain_float_cast),
+            contract_rows(back_all, active).astype(brain_float_cast),
+        ],
+        axis=1,
+    )
+    grad_ffn, grad_normed_two = lax.optimization_barrier((grad_ffn, grad_normed_two))
+    owned_ffn = lax.psum_scatter(grad_ffn, "dp", scatter_dimension=0, tiled=True).astype(
+        single_precision
+    )
     grad_gain_two = jnp.sum(grad_normed_two * base_two, axis=0)
     scaled_two = grad_normed_two * gain_all[1]
     grad_hidden = grad_out + scale_two * (
@@ -281,14 +319,14 @@
         grad_value_heads.append(jnp.concatenate(value_parts, axis=0))
     grad_key_all = jnp.concatenate(grad_key_heads, axis=1)
     grad_value_all = jnp.concatenate(grad_value_heads, axis=1)
-    key_gradient, grad_value = (
-        lax.psum_scatter(
-            grad_key_all.astype(jnp.bfloat16), "mp", scatter_dimension=0, tiled=True
-        ).astype(jnp.float32),
-        lax.psum_scatter(
-            grad_value_all.astype(jnp.bfloat16), "mp", scatter_dimension=0, tiled=True
-        ).astype(jnp.float32),
-    )
+    key_value_gradient = lax.psum_scatter(
+        jnp.concatenate([grad_key_all, grad_value_all], axis=1).astype(jnp.bfloat16),
+        "mp",
+        scatter_dimension=0,
+        tiled=True,
+    ).astype(jnp.float32)
+    key_gradient = key_value_gradient[:, : KEY_VALUE_HEADS * HEAD_SIZE]
+    grad_value = key_value_gradient[:, KEY_VALUE_HEADS * HEAD_SIZE :]
     grad_query_all = jnp.stack(grad_query_heads, axis=1).reshape(token_rows, QUERY_HEADS, HEAD_SIZE)
     grad_query_all = rotation_backward(grad_query_all, cosine_table, sine_lookup).reshape(
         token_rows, QUERY_WIDTH
@@ -308,21 +346,31 @@
         scaled_one - base_one * jnp.mean(scaled_one * base_one, axis=-1, keepdims=True)
     )
     input_grad = grad_inputs.astype(brain_float_cast)
-    grad_gains = jnp.stack([grad_gain_one, grad_gain_two], axis=0)
-    grad_qkv_w, grad_out_w, grad_bias, grad_gains = (
-        lax.psum(grad_qkv_w.astype(jnp.bfloat16), "mp").astype(jnp.float32),
-        lax.psum(grad_out_w.astype(jnp.bfloat16), "mp").astype(jnp.float32),
-        lax.psum(grad_bias.astype(jnp.bfloat16), "mp").astype(jnp.float32),
-        lax.psum(grad_gains.astype(jnp.bfloat16), "mp").astype(jnp.float32),
-    )
-    owned_qkv, owned_out, owned_bias, owned_gains, owned_gate_up, owned_down = (
-        lax.psum_scatter(grad_qkv_w, "dp", scatter_dimension=0, tiled=True),
-        lax.psum_scatter(grad_out_w, "dp", scatter_dimension=0, tiled=True),
-        lax.psum_scatter(grad_bias, "dp", scatter_dimension=0, tiled=True),
-        lax.psum_scatter(grad_gains, "dp", scatter_dimension=1, tiled=True),
-        lax.psum_scatter(grad_gate_up, "dp", scatter_dimension=0, tiled=True),
-        lax.psum_scatter(grad_down, "dp", scatter_dimension=1, tiled=True),
-    )
+    grad_attention = jnp.concatenate([grad_qkv_w, grad_out_w], axis=1).astype(brain_float_cast)
+    grad_attention = lax.psum_scatter(grad_attention, "mp", scatter_dimension=1, tiled=True)
+    grad_attention = lax.psum_scatter(grad_attention, "dp", scatter_dimension=0, tiled=True)
+    grad_attention = lax.all_gather(grad_attention, "mp", axis=1, tiled=True).astype(
+        single_precision
+    )
+    owned_qkv = grad_attention[:, :QKV]
+    owned_out = grad_attention[:, QKV:]
+    grad_vectors = jnp.concatenate(
+        [
+            grad_bias.reshape(-1, owned_width),
+            grad_gain_one.reshape(-1, gain_width),
+            grad_gain_two.reshape(-1, gain_width),
+        ],
+        axis=1,
+    )
+    owned_vectors = lax.dynamic_index_in_dim(
+        lax.psum(grad_vectors, ("dp", "mp")), lax.axis_index("dp"), keepdims=False
+    )
+    owned_bias = owned_vectors[:owned_width]
+    owned_gains = owned_vectors[owned_width:].reshape(2, gain_width)
+    owned_gate_up = jnp.stack(
+        [owned_ffn[:, :width_ff], owned_ffn[:, width_ff : 2 * width_ff]], axis=1
+    )
+    owned_down = owned_ffn[:, 2 * width_ff :].T
     upd_qkv = adam_update(qkv_weight, owned_qkv, qkv_moment, qkv_square, 1.5 * D ** (-0.5), 0.1)
     upd_bias = adam_update(qkv_bias, owned_bias, bias_moment, bias_square, 0.3, 0.0)
     upd_out = adam_update(

time: 1350 us -> 931 us (0.69)
  waiting for transfers between devices: 765 us -> 398 us
  blocking collectives: 83.4 us -> 46.8 us
  matrix products: 256 us -> 237 us
  other arithmetic: 75.8 us -> 93.9 us
  local copies, waits for them, and re-layouts: 144 us -> 126 us
    unnamed x18 -> x12, waiting for transfers between devices: 326 us -> 1.21 us
    reduce_scatter x7 -> x6, waiting for transfers between devices: 344 us -> 204 us  [the longest x1 115 us: per_device(): lax.psum_scatter(grad_ffn, 'dp', scatter_dimension=0, tiled=True)]
    all_gather x3, waiting for transfers between devices: 36.4 us -> 156 us  [the longest x1 106 us: per_device(): lax.all_gather(jnp.concatenate([gate_up_weight[:, 0], gate_up_weight[:, 1...]
    unnamed x2 -> x0, blocking collectives: 40.3 us -> none
    psum x1, blocking collectives: 6.46 us -> 39.8 us  [per_device(): lax.psum(grad_vectors, ('dp', 'mp'))]
    all_gather x3 -> x1, blocking collectives: 36.6 us -> 7.01 us  [per_device(): lax.all_gather(grad_attention, 'mp', axis=1, tiled=True)]
    concatenate x2 -> x7, other arithmetic: 1.7 us -> 29.8 us  [the longest x1 11.6 us: per_device(): jnp.concatenate([grad_key_all, grad_value_all], axis=1).astype(jnp.bfloat16)]
    dot_general x20, matrix products: 109 us -> 83.9 us  [contract_cols(): lax.dot_general(left, right, (((1,), (1,)), ((), ())), preferred_element_...]
  transfers between devices with their start and end apart: 16 -> 12, of which waited for: 12 -> 8; matrix products, arithmetic and copies ran while one was open for 24% -> 28% of each run, Pallas kernels for 0% -> 0%
where the time goes in v1:
time: 931 us; the launch traced here: 919 us
  waiting for transfers between devices  398 us (43%)
  matrix products  237 us (25%)
  local copies, waits for them, and re-layouts  126 us (14%)
  other arithmetic  93.9 us (10%)
  blocking collectives  46.8 us (5%)
  between operations  16.2 us (2%)
    reduce_scatter x1, waiting for transfers between devices, per_device(): lax.psum_scatter(grad_ffn, 'dp', scatter_dimension=0, tiled=True)  115 us
    all_gather x1, waiting for transfers between devices, per_device(): lax.all_gather(jnp.concatenate([gate_up_weight[:, 0], gate_up_weight[:, 1...  106 us
    dot_general x20, matrix products, contract_cols(): lax.dot_general(left, right, (((1,), (1,)), ((), ())), preferred_element_...  83.9 us
    dot_general x20, matrix products, contract_rows(): lax.dot_general(left, right, (((0,), (0,)), ((), ())), preferred_element_...  73.7 us
    all_gather x1, waiting for transfers between devices, per_device(): lax.all_gather(jnp.concatenate([qkv_weight.astype(brain_float_cast), pack...  50.3 us
    reduce_scatter x1, waiting for transfers between devices, per_device(): lax.psum_scatter(grad_attention, 'mp', scatter_dimension=1, tiled=True)  41.8 us
    psum x1, blocking collectives, per_device(): lax.psum(grad_vectors, ('dp', 'mp'))  39.8 us
    reduce_scatter x1, waiting for transfers between devices, per_device(): lax.psum_scatter(contract_cols(active, w_down_t).astype(jnp.bfloat16), 'm...  36.6 us
  transfers between devices with their start and end apart: 12, of which 8 were waited for; matrix products, arithmetic and copies ran while one was open for 28% of the time, Pallas kernels for 0%

profile of v1, /device:TPU:0, one launch (start us, length us, event | category | flops | bytes accessed | tf_op | source)
XLA Modules:
  0.0 919.1 jit_solution(3967778302202637060)
XLA Ops:
  15.3 50.3 %all-gather.7.cloned.1.call-done = bf16[896,1280]{1,0:T(8,128)(2,1)} async-done(((bf16[112,1280]{1,0:T(8,128)(2,1)}), bf16[896,1280]{1,0:T(8,128)(2,1)}) %all-gather.7.cloned.1.call-update) | async-done | bytes 2293776 | tf_op jit(solution)/shard_map/all_gather | solution.py:108
  149.0 7.2 select_reduce_fusion.7
  156.1 8.2 select_reduce_fusion.6
  224.9 23.2 %all-gather.13.cloned.1.call-done = bf16[2048,896]{1,0:T(8,128)(2,1)} async-done(((bf16[512,896]{1,0:T(8,128)(2,1)}), bf16[2048,896]{1,0:T(8,128)(2,1)}) %all-gather.13.cloned.1.call-update) | async-done | bytes 3670032 | tf_op jit(solution)/shard_map/all_gather | solution.py:227
  248.1 106.1 %all-gather.15.cloned.1.call-done = bf16[896,3648]{1,0:T(8,128)(2,1)} async-done(((bf16[112,3648]{1,0:T(8,128)(2,1)}), bf16[896,3648]{1,0:T(8,128)(2,1)}) %all-gather.15.cloned.1.call-update) | async-done | bytes 6537232 | tf_op jit(solution)/shard_map/all_gather | solution.py:124
  354.2 17.5 %fusion.17 = f32[2048,2432]{1,0:T(8,128)} fusion(bf16[2048,896]{1,0:T(8,128)(2,1)} %all-gather.13.cloned.1.call-done, bf16[896,3648]{1,0:T(8,128)(2,1)} %all-gather.15.cloned.1.call-done), kind=kOutput, calls=%fused_computation.69 | convolution fusion | flops 8925478912 | bytes 27951104 | tf_op jit(solution)/shard_map/dot_general | solution.py:230
  371.8 13.5 %all-gather.17.cloned.1.call-done = bf16[2048,896]{1,0:T(8,128)(2,1)} async-done(((bf16[512,896]{1,0:T(8,128)(2,1)}), bf16[2048,896]{1,0:T(8,128)(2,1)}) %all-gather.17.cloned.1.call-update) | async-done | bytes 3670032 | tf_op jit(solution)/shard_map/all_gather | solution.py:132
  385.3 17.8 %fusion.2 = (bf16[2048,1216]{1,0:T(8,128)(2,1)}, bf16[2048,1216]{1,0:T(8,128)(2,1)}, bf16[2048,1216]{1,0:T(8,128)(2,1)}) fusion(f32[2048,2432]{1,0:T(8,128)} %fusion.17, bf16[2048,896]{1,0:T(8,128)(2,1)} %all-gather.17.cloned.1.call-done, bf16[896,3648]{1,0:T(8,128)(2,1)} %all-gather.15.cloned.1.call-done), kind=kOutput, calls=%fused_computation.4 | convolution fusion | flops 4500094976 | bytes 41877504 | tf_op jit(solution)/shard_map/dot_general | solution.py:237
  403.1 8.0 pad_maximum_fusion
  414.9 12.3 %fusion.19 = bf16[2048,896]{1,0:T(8,128)(2,1)} fusion(bf16[2048,2432]{1,0:T(8,128)(2,1)S(1)} %pad_maximum_fusion, bf16[896,3648]{1,0:T(8,128)(2,1)S(1)} %copy-done.97), kind=kOutput, calls=%fused_computation.72 | convolution fusion | flops 8927313920 | bytes 17989632 | tf_op jit(solution)/shard_map/dot_general | solution.py:53
  427.3 9.9 %convolution_convert_fusion.3 = bf16[2048,896]{1,0:T(8,128)(2,1)} fusion(bf16[2048,1216]{1,0:T(8,128)(2,1)} %get-tuple-element.30, bf16[896,3648]{1,0:T(8,128)(2,1)} %all-gather.15.cloned.1.call-done), kind=kOutput, calls=%fused_computation.75 | convolution fusion | flops 4464574464 | bytes 11206656 | tf_op jit(solution)/shard_map/dot_general | solution.py:53
  437.3 10.5 %fusion.22 = bf16[896,1216]{0,1:T(8,128)(2,1)} fusion(bf16[2048,1216]{1,0:T(8,128)(2,1)} %get-tuple-element.30, bf16[2048,896]{1,0:T(8,128)(2,1)} %all-gather.17.cloned.1.call-done), kind=kOutput, calls=%fused_computation.77 | convolution fusion | flops 4463828992 | bytes 10829824 | tf_op jit(solution)/shard_map/dot_general | solution.py:47
  452.1 15.2 %convolution_convert_fusion = bf16[896,2432]{1,0:T(8,128)(2,1)} fusion(bf16[2048,896]{1,0:T(8,128)(2,1)} %all-gather.13.cloned.1.call-done, bf16[2048,2432]{1,0:T(8,128)(2,1)} %copy-done.51), kind=kOutput, calls=%fused_computation.43 | convolution fusion | flops 8927657984 | bytes 17989632 | tf_op jit(solution)/shard_map/dot_general | solution.py:47
  476.1 36.6 %reduce-scatter.7.cloned.1.call-done = bf16[512,896]{1,0:T(8,128)(2,1)} async-done(((bf16[2048,896]{1,0:T(8,128)(2,1)}), bf16[512,896]{1,0:T(8,128)(2,1)}) %reduce-scatter.7.cloned.1.call-update) | async-done | bytes 917520 | tf_op jit(solution)/shard_map/reduce_scatter | solution.py:250
  529.9 6.2 convolution_convert_fusion.13
  536.2 5.6 convolution_convert_fusion.12
  551.9 6.2 convolution_convert_fusion.9
  569.9 6.5 multiply_convert_fusion.8
  615.9 11.6 %maximum_maximum_fusion = bf16[2048,256]{0,1:T(8,128)(2,1)} fusion(bf16[512,64]{0,1:T(8,128)(2,1)S(1)} %copy-done.90, bf16[512,64]{0,1:T(8,128)(2,1)S(1)} %copy-done.89, bf16[512,64]{0,1:T(8,128)(2,1)S(1)} %copy-done.88, bf16[512,64]{0,1:T(8,128)(2,1)S(1)} %copy-done.87, bf16[512,64]{0,1:T(8,128)(2,1)S(1)} %copy-done.86, bf16[512,64]{0,1:T(8,128)(2,1)S(1)} %copy-done.85, ...), kind=kLoop, calls=%fused_computation.145 | loop fusion | flops 16777216 | bytes 2097152 | tf_op jit(solution)/shard_map/concatenate | solution.py:323
  666.4 41.8 %reduce-scatter.13.cloned.1.call-done = bf16[896,512]{1,0:T(8,128)(2,1)} async-done(((bf16[896,2048]{1,0:T(8,128)(2,1)}), bf16[896,512]{1,0:T(8,128)(2,1)}) %reduce-scatter.13.cloned.1.call-update) | async-done | bytes 917520 | tf_op jit(solution)/shard_map/reduce_scatter | solution.py:350
  717.4 39.8 %psum.7 = f32[8,368]{1,0:T(8,128)S(1)} all-reduce(f32[8,368]{1,0:T(8,128)S(1)} %pad_maximum_fusion.13), channel_id=1, replica_groups=mesh['dp'=8,'mp'=4] {'dp','mp'}, use_global_device_ids=true, to_apply=%region_30.31 | all-reduce | flops 2944 | bytes 23552 | tf_op jit(solution)/shard_map/psum | solution.py:366
  763.9 10.5 %reduce-scatter.15.cloned.1.call-done = bf16[112,512]{1,0:T(8,128)(2,1)} async-done(((bf16[896,512]{1,0:T(8,128)(2,1)}), bf16[112,512]{1,0:T(8,128)(2,1)}) %reduce-scatter.15.cloned.1.call-update) | async-done | bytes 114704 | tf_op jit(solution)/shard_map/reduce_scatter | solution.py:351
  774.5 7.0 all_gather.27
  785.4 115.3 %reduce-scatter.17.cloned.1.call-done = bf16[112,3648]{1,0:T(8,128)(2,1)} async-done(((bf16[896,3648]{1,0:T(8,128)(2,1)}), bf16[112,3648]{1,0:T(8,128)(2,1)}) %reduce-scatter.17.cloned.1.call-update) | async-done | bytes 817168 | tf_op jit(solution)/shard_map/reduce_scatter | solution.py:265
  (471 shorter events, 316.1 us)
Async XLA Ops:
  7.2 59.8 %copy-start.60 = (bf16[512,896]{1,0:T(8,128)(2,1)S(1)}, bf16[512,896]{1,0:T(8,128)(2,1)}, u32[]{:S(2)}) copy-start(bf16[512,896]{1,0:T(8,128)(2,1)} %param.21) | copy-start | bytes 2752516
  7.2 58.4 %all-gather.7.cloned.1.call-start = ((), (), s32[]{:S(2)}) async-start(), calls=%async_computation.6 | async-start | bytes 2580480 | tf_op jit(solution)/shard_map/all_gather | solution.py:108
  11.5 108.8 %all-gather.9.cloned.1.call-start = ((), (), s32[]{:S(2)}) async-start(), calls=%async_computation.7 | async-start | bytes 1310720 | tf_op jit(solution)/shard_map/all_gather | solution.py:167
  15.0 55.2 %copy-start.93 = (f32[512]{0:T(512)}, f32[512]{0:T(512)S(1)}, u32[]{:S(2)}) copy-start(f32[512]{0:T(512)S(1)} %add_rsqrt_fusion.1) | copy-start | bytes 6148
  15.3 95.9 %copy-start.65 = (f32[512,32]{0,1:T(8,128)}, f32[512,32]{0,1:T(8,128)S(1)}, u32[]{:S(2)}) copy-start(f32[512,32]{0,1:T(8,128)S(1)} %get-tuple-element.268) | copy-start | bytes 196612
  15.3 95.9 %copy-start.67 = (f32[512,32]{0,1:T(8,128)}, f32[512,32]{0,1:T(8,128)S(1)}, u32[]{:S(2)}) copy-start(f32[512,32]{0,1:T(8,128)S(1)} %get-tuple-element.269) | copy-start | bytes 196612
  72.7 140.8 %all-gather.11.cloned.1.call-start = ((), (), s32[]{:S(2)}) async-start(), calls=%async_computation.8 | async-start | bytes 1806336 | tf_op jit(solution)/shard_map/all_gather | solution.py:123
  73.5 174.6 %all-gather.13.cloned.1.call-start = ((), (), s32[]{:S(2)}) async-start(), calls=%async_computation.9 | async-start | bytes 4587520 | tf_op jit(solution)/shard_map/all_gather | solution.py:227
  123.9 59.3 %copy-start = (f32[3584,512]{0,1:T(8,128)}, f32[3584,512]{0,1:T(8,128)S(1)}, u32[]{:S(2)}) copy-start(f32[3584,512]{0,1:T(8,128)S(1)} %get-tuple-element.281) | copy-start | bytes 22020100
  126.8 54.7 %copy-start.2 = (f32[3584,512]{0,1:T(8,128)}, f32[3584,512]{0,1:T(8,128)S(1)}, u32[]{:S(2)}) copy-start(f32[3584,512]{0,1:T(8,128)S(1)} %get-tuple-element.283) | copy-start | bytes 22020100
  218.0 136.2 %all-gather.15.cloned.1.call-start = ((), (), s32[]{:S(2)}) async-start(), calls=%async_computation.10 | async-start | bytes 7483392 | tf_op jit(solution)/shard_map/all_gather | solution.py:124
  224.3 161.0 %all-gather.17.cloned.1.call-start = ((), (), s32[]{:S(2)}) async-start(), calls=%async_computation.11 | async-start | bytes 4587520 | tf_op jit(solution)/shard_map/all_gather | solution.py:132
  224.9 248.0 %reduce-scatter.9.cloned.1.call-start = ((), (), s32[]{:S(2)}) async-start(), calls=%async_computation.13 | async-start | bytes 4587520 | tf_op jit(solution)/shard_map/reduce_scatter | solution.py:244
  427.2 85.4 %reduce-scatter.7.cloned.1.call-start = ((), (), s32[]{:S(2)}) async-start(), calls=%async_computation.12 | async-start | bytes 4587520 | tf_op jit(solution)/shard_map/reduce_scatter | solution.py:250
  437.2 222.8 %reduce-scatter.11.cloned.1.call-start = ((), (), s32[]{:S(2)}) async-start(), calls=%async_computation.14 | async-start | bytes 1310720 | tf_op jit(solution)/shard_map/reduce_scatter | solution.py:322
  627.6 80.6 %reduce-scatter.13.cloned.1.call-start = ((), (), s32[]{:S(2)}) async-start(), calls=%async_computation.15 | async-start | bytes 4587520 | tf_op jit(solution)/shard_map/reduce_scatter | solution.py:350
  666.3 108.1 %reduce-scatter.15.cloned.1.call-start = ((), (), s32[]{:S(2)}) async-start(), calls=%async_computation.16 | async-start | bytes 1032192 | tf_op jit(solution)/shard_map/reduce_scatter | solution.py:351
  708.2 192.5 %reduce-scatter.17.cloned.1.call-start = ((), (), s32[]{:S(2)}) async-start(), calls=%async_computation.17 | async-start | bytes 7483392 | tf_op jit(solution)/shard_map/reduce_scatter | solution.py:265
  715.7 65.8 %copy-start.71 = (f32[112,896]{1,0:T(8,128)S(1)}, f32[112,896]{1,0:T(8,128)}, u32[]{:S(2)}) copy-start(f32[112,896]{1,0:T(8,128)} %param.30) | copy-start | bytes 1204228
  715.7 65.8 %copy-start.81 = (f32[112,896]{1,0:T(8,128)S(1)}, f32[112,896]{1,0:T(8,128)}, u32[]{:S(2)}) copy-start(f32[112,896]{1,0:T(8,128)} %param.32) | copy-start | bytes 1204228
  715.7 65.8 %copy-start.82 = (f32[112,896]{1,0:T(8,128)S(1)}, f32[112,896]{1,0:T(8,128)}, u32[]{:S(2)}) copy-start(f32[112,896]{1,0:T(8,128)} %param.31) | copy-start | bytes 1204228
  782.7 119.4 %copy-start.58 = (f32[112,2,1216]{2,1,0:T(2,128)S(1)}, f32[112,2,1216]{2,1,0:T(2,128)}, u32[]{:S(2)}) copy-start(f32[112,2,1216]{2,1,0:T(2,128)} %param.33) | copy-start | bytes 3268612
  782.7 119.4 %copy-start.72 = (f32[112,2,1216]{2,1,0:T(2,128)S(1)}, f32[112,2,1216]{2,1,0:T(2,128)}, u32[]{:S(2)}) copy-start(f32[112,2,1216]{2,1,0:T(2,128)} %param.35) | copy-start | bytes 3268612
  785.4 116.8 %copy-start.73 = (f32[112,2,1216]{2,1,0:T(2,128)S(1)}, f32[112,2,1216]{2,1,0:T(2,128)}, u32[]{:S(2)}) copy-start(f32[112,2,1216]{2,1,0:T(2,128)} %param.34) | copy-start | bytes 3268612
  (115 other events, 712.1 us)
Sparse Core Ops, SparseCore 0:
  11.6 53.9 all-gather.6
  72.9 15.2 all-gather.8
  90.9 44.2 all-gather.10
  218.1 29.9 all-gather.12
  250.7 103.5 all-gather.14
  355.7 29.5 all-gather.16
  427.4 41.2 reduce-scatter.8
  471.3 41.2 reduce-scatter.6
  627.7 24.8 reduce-scatter.10
  666.5 41.6 reduce-scatter.12
  711.5 62.9 reduce-scatter.14
  778.3 122.2 reduce-scatter.16

commit v2 on v1

--- a/solution.py
+++ b/solution.py
@@ -1,6 +1,8 @@
 import jax
 import jax.numpy as jnp
 from jax import lax
+from jax.experimental import pallas as pl
+from jax.experimental.pallas import tpu as pltpu
 from jax.sharding import PartitionSpec as P
 
 D = 896
@@ -21,28 +23,6 @@
 MASKED = -1e30
 
 
-def apply_rotation(values, cosine_table, sine_lookup):
-    half_dim = values.shape[-1] // 2
-    first_half = values[..., :half_dim]
-    second = values[..., half_dim:]
-    cos_b = cosine_table[:, None, :]
-    sin_b = sine_lookup[:, None, :]
-    return jnp.concatenate(
-        [first_half * cos_b - second * sin_b, second * cos_b + first_half * sin_b], axis=-1
-    )
-
-
-def rotation_backward(values, cosine_table, sine_lookup):
-    half_dim = values.shape[-1] // 2
-    first_half = values[..., :half_dim]
-    second = values[..., half_dim:]
-    cos_b = cosine_table[:, None, :]
-    sin_b = sine_lookup[:, None, :]
-    return jnp.concatenate(
-        [first_half * cos_b + second * sin_b, second * cos_b - first_half * sin_b], axis=-1
-    )
-
-
 def contract_rows(left, right):
     return lax.dot_general(
         left, right, (((0,), (0,)), ((), ())), preferred_element_type=jnp.float32
@@ -53,6 +33,137 @@
     return lax.dot_general(
         left, right, (((1,), (1,)), ((), ())), preferred_element_type=jnp.float32
     )
+
+
+def swap_halves(values):
+    lane = lax.broadcasted_iota(jnp.int32, values.shape, 1) % HEAD_SIZE
+    return jnp.where(
+        lane < HEAD_SIZE // 2,
+        pltpu.roll(values, 128 - HEAD_SIZE // 2, 1),
+        pltpu.roll(values, HEAD_SIZE // 2, 1),
+    )
+
+
+def attention_forward_kernel(
+    place, qkv_ref, cos_ref, sin_ref, start_ref, k_ref, v_ref, q_out, o_out, log_out
+):
+    rows = qkv_ref.shape[0]
+    pair = pl.program_id(0)
+    own = place[0]
+    x = qkv_ref[...]
+    rotated = (x * cos_ref[...] + swap_halves(x) * sin_ref[...]).astype(jnp.bfloat16)
+    q_out[...] = rotated
+    heads = (rotated[:, :HEAD_SIZE], rotated[:, HEAD_SIZE:])
+    starts = start_ref[...]
+    query = own * rows + lax.broadcasted_iota(jnp.int32, (rows, rows), 0)
+
+    def step(block, carry):
+        at = pl.ds(pl.multiple_of(block * rows, rows), rows)
+        key = block * rows + lax.broadcasted_iota(jnp.int32, (rows, rows), 1)
+        allowed = (key <= query) & (key >= starts)
+        result = []
+        for half in range(2):
+            top, total, acc = carry[half]
+            kv = (pair * 2 + half) // (QUERY_HEADS // KEY_VALUE_HEADS)
+            scores = contract_cols(heads[half], k_ref[kv, at, :]) * HEAD_SIZE**-0.5
+            scores = jnp.where(allowed, scores, MASKED)
+            new_top = jnp.maximum(top, jnp.max(scores, axis=1, keepdims=True))
+            weights = jnp.exp(scores - new_top)
+            fade = jnp.exp(top - new_top)
+            total = total * fade + jnp.sum(weights, axis=1, keepdims=True)
+            acc = acc * fade + jnp.dot(
+                weights.astype(jnp.bfloat16), v_ref[kv, at, :], preferred_element_type=jnp.float32
+            )
+            result.append((new_top, total, acc))
+        return tuple(result)
+
+    empty = (
+        jnp.full((rows, 1), MASKED, jnp.float32),
+        jnp.zeros((rows, 1), jnp.float32),
+        jnp.zeros((rows, HEAD_SIZE), jnp.float32),
+    )
+    done = lax.fori_loop(place[1], own + 1, step, (empty, empty))
+    o_out[...] = jnp.concatenate([acc / total for _, total, acc in done], axis=1)
+    log_out[...] = jnp.concatenate(
+        [jnp.broadcast_to(top + jnp.log(total), (rows, HEAD_SIZE)) for top, total, _ in done],
+        axis=1,
+    )
+
+
+def attention_backward_kernel(
+    place, q_ref, do_ref, o_ref, log_ref, cos_ref, sin_ref, start_ref, k_ref, v_ref, dq_out, dk_out, dv_out
+):
+    rows = q_ref.shape[0]
+    pair = pl.program_id(0)
+    own = place[0]
+
+    @pl.when(pair == 0)
+    def _():
+        dk_out[...] = jnp.zeros_like(dk_out)
+        dv_out[...] = jnp.zeros_like(dv_out)
+
+    q = q_ref[...]
+    do = do_ref[...]
+    log_rows = log_ref[...].T
+    products = (do.astype(jnp.float32) * o_ref[...]).T
+    starts = start_ref[...]
+    query = own * rows + lax.broadcasted_iota(jnp.int32, (rows, rows), 1)
+
+    def step(block, carry):
+        at = pl.ds(pl.multiple_of(block * rows, rows), rows)
+        key = block * rows + lax.broadcasted_iota(jnp.int32, (rows, rows), 0)
+        allowed = (key <= query) & (key >= starts)
+        result = []
+        for half in range(2):
+            lanes = slice(half * HEAD_SIZE, (half + 1) * HEAD_SIZE)
+            kv = (pair * 2 + half) // (QUERY_HEADS // KEY_VALUE_HEADS)
+            k = k_ref[kv, at, :]
+            log_total = log_rows[half * HEAD_SIZE : half * HEAD_SIZE + 1]
+            delta = jnp.sum(products[lanes], axis=0, keepdims=True)
+            scores = contract_cols(k, q[:, lanes]) * HEAD_SIZE**-0.5
+            weights = jnp.exp(jnp.where(allowed, scores - log_total, MASKED))
+            dv_out[kv, at, :] += jnp.dot(
+                weights.astype(jnp.bfloat16), do[:, lanes], preferred_element_type=jnp.float32
+            )
+            grad = contract_cols(v_ref[kv, at, :], do[:, lanes])
+            grad = (weights * (grad - delta)).astype(jnp.bfloat16)
+            dk_out[kv, at, :] += jnp.dot(
+                grad, q[:, lanes], preferred_element_type=jnp.float32
+            ) * HEAD_SIZE**-0.5
+            result.append(carry[half] + contract_rows(grad, k))
+        return tuple(result)
+
+    empty = jnp.zeros((rows, HEAD_SIZE), jnp.float32)
+    done = lax.fori_loop(place[1], own + 1, step, (empty, empty))
+    dq = jnp.concatenate(done, axis=1) * HEAD_SIZE**-0.5
+    dq_out[...] = (dq * cos_ref[...] - swap_halves(dq) * sin_ref[...]).astype(jnp.bfloat16)
+
+
+def column_block(rows):
+    return pl.BlockSpec((rows, 128), lambda j, place: (0, j))
+
+
+def whole_block(array):
+    return pl.BlockSpec(array.shape, lambda j, place: (0,) * array.ndim)
+
+
+def attention_call(kernel, place, blocked, whole, outs, whole_outs, factor):
+    rows = blocked[0].shape[0]
+    work = QUERY_HEADS * rows * whole[-1].shape[1]
+    return pl.pallas_call(
+        kernel,
+        grid_spec=pltpu.PrefetchScalarGridSpec(
+            num_scalar_prefetch=1,
+            grid=(QUERY_WIDTH // 128,),
+            in_specs=[column_block(rows) for _ in blocked] + [whole_block(a) for a in whole],
+            out_specs=[column_block(rows) for _ in outs] + [whole_block(a) for a in whole_outs],
+        ),
+        out_shape=[jax.ShapeDtypeStruct((rows, QUERY_WIDTH), t) for t in outs] + list(whole_outs),
+        compiler_params=pltpu.CompilerParams(vmem_limit_bytes=40 * 2**20),
+        cost_estimate=pl.CostEstimate(
+            flops=factor * work * 256, bytes_accessed=8 * 2**20, transcendentals=work
+        ),
+    )(place, *blocked, *whole)
 
 
 def adam_update(weight, gradient, moment, square, step_rate, decay_rate):
@@ -92,11 +203,8 @@
     brain_float_cast = jnp.bfloat16
     single_precision = jnp.float32
     token_rows = tokens.shape[0]
-    axis_parts = lax.axis_size("mp")
     own_index = lax.axis_index("mp")
-    group_of_heads = QUERY_HEADS // KEY_VALUE_HEADS
     width_ff = down_weight.shape[0]
-    score_scale = HEAD_SIZE ** (-0.5)
     owned_width = qkv_bias.shape[0]
     gain_width = norm_gains.shape[1]
     owned_rows = qkv_weight.shape[0]
@@ -146,79 +254,41 @@
     angles = position.astype(single_precision)[:, None] * inverse[None, :]
     cosine_table = jnp.cos(angles)
     sine_lookup = jnp.sin(angles)
-    rotated_queries = apply_rotation(
-        query_key_value[:, :QUERY_WIDTH].reshape(token_rows, QUERY_HEADS, HEAD_SIZE),
-        cosine_table,
-        sine_lookup,
-    ).astype(brain_float_cast)
-    rotated_keys = apply_rotation(
-        query_key_value[:, QUERY_WIDTH : QUERY_WIDTH + KEY_VALUE_HEADS * HEAD_SIZE].reshape(
-            token_rows, KEY_VALUE_HEADS, HEAD_SIZE
-        ),
-        cosine_table,
-        sine_lookup,
-    )
-    rotated_keys = rotated_keys.astype(brain_float_cast).reshape(
-        token_rows, KEY_VALUE_HEADS * HEAD_SIZE
-    )
+    cosine_lanes = jnp.tile(cosine_table, (1, 4))
+    sine_lanes = jnp.tile(jnp.concatenate([-sine_lookup, sine_lookup], axis=1), (1, 2))
+
+    def swapped(values):
+        half = HEAD_SIZE // 2
+        return jnp.concatenate(
+            [values[:, (p ^ 1) * half : (p ^ 1) * half + half] for p in range(2 * KEY_VALUE_HEADS)],
+            axis=1,
+        )
+
+    keys = query_key_value[:, QUERY_WIDTH : QUERY_WIDTH + KEY_VALUE_HEADS * HEAD_SIZE]
+    rotated_keys = (keys * cosine_lanes + swapped(keys) * sine_lanes).astype(brain_float_cast)
     value_matrix = query_key_value[:, QUERY_WIDTH + KEY_VALUE_HEADS * HEAD_SIZE :].astype(
         brain_float_cast
     )
     key_value_all = lax.all_gather(
         jnp.concatenate([rotated_keys, value_matrix], axis=1), "mp", axis=0, tiled=True
     )
-    key_all = key_value_all[:, : KEY_VALUE_HEADS * HEAD_SIZE]
-    value_all = key_value_all[:, KEY_VALUE_HEADS * HEAD_SIZE :]
-    allowed_list = []
-    for source in range(axis_parts):
-        key_index = source * token_rows + jnp.arange(token_rows, dtype=jnp.int32)
-        key_seg = segrow[source * token_rows : (source + 1) * token_rows]
-        allowed = (key_index[None, :] <= query_index[:, None]) & (
-            key_seg[None, :] == own_seg[:, None]
-        )
-        allowed_list.append(jnp.repeat(allowed, group_of_heads, axis=0))
-
-    def block_scores(q_block, key_value_head, source):
-        key_block = key_all[
-            source * token_rows : (source + 1) * token_rows,
-            key_value_head * HEAD_SIZE : (key_value_head + 1) * HEAD_SIZE,
-        ]
-        raw_scores = contract_cols(q_block, key_block) * score_scale
-        return jnp.where(allowed_list[source], raw_scores, MASKED)
-
-    query_list = []
-    log_totals = []
-    head_outputs = []
-    for key_value_head in range(KEY_VALUE_HEADS):
-        q_block = rotated_queries[
-            :, key_value_head * group_of_heads : (key_value_head + 1) * group_of_heads, :
-        ].reshape(token_rows * group_of_heads, HEAD_SIZE)
-        query_list.append(q_block)
-        row_top = jnp.full((token_rows * group_of_heads,), MASKED, single_precision)
-        row_total = jnp.zeros((token_rows * group_of_heads,), single_precision)
-        for source in range(axis_parts):
-            scores = block_scores(q_block, key_value_head, source)
-            new_top = jnp.maximum(row_top, jnp.max(scores, axis=-1))
-            shifted = jnp.where(allowed_list[source], jnp.exp(scores - new_top[:, None]), 0.0)
-            row_total = row_total * jnp.exp(row_top - new_top) + jnp.sum(shifted, axis=-1)
-            row_top = new_top
-        log_total = row_top + jnp.log(row_total)
-        log_totals.append(log_total)
-        attended_part = jnp.zeros((token_rows * group_of_heads, HEAD_SIZE), single_precision)
-        for source in range(axis_parts):
-            scores = block_scores(q_block, key_value_head, source)
-            prob_block = jnp.where(
-                allowed_list[source], jnp.exp(scores - log_total[:, None]), 0.0
-            ).astype(brain_float_cast)
-            value_block = value_all[
-                source * token_rows : (source + 1) * token_rows,
-                key_value_head * HEAD_SIZE : (key_value_head + 1) * HEAD_SIZE,
-            ]
-            attended_part = attended_part + jnp.dot(
-                prob_block, value_block, preferred_element_type=single_precision
-            )
-        head_outputs.append(attended_part.reshape(token_rows, group_of_heads, HEAD_SIZE))
-    attention_output = jnp.stack(head_outputs, axis=1).reshape(token_rows, QUERY_WIDTH)
+    sequence = key_value_all.shape[0]
+    heads_first = key_value_all.reshape(sequence, 2 * KEY_VALUE_HEADS, HEAD_SIZE).swapaxes(0, 1)
+    key_heads = heads_first[:KEY_VALUE_HEADS]
+    value_heads = heads_first[KEY_VALUE_HEADS:]
+    place = jnp.stack([own_index, before[0] // token_rows]).astype(jnp.int32)
+    rotated_queries, attention_output, log_totals = attention_call(
+        attention_forward_kernel,
+        place,
+        [query_key_value],
+        [cosine_lanes, sine_lanes, before[:, None], key_heads, value_heads],
+        [brain_float_cast, single_precision, single_precision],
+        [],
+        1,
+    )
+    attention_output, w_ffn, back_all, w_out = lax.optimization_barrier(
+        (attention_output, w_ffn, back_all, w_out)
+    )
     attended_low = attention_output.astype(brain_float_cast)
     hidden = inputs + jnp.dot(attended_low, w_out, preferred_element_type=single_precision)
     scale_two = lax.rsqrt(jnp.mean(hidden * hidden, axis=-1, keepdims=True) + NORM_EPS)
@@ -273,52 +343,23 @@
     grad_branch = grad_hidden.astype(brain_float_cast)
     grad_out_w = contract_rows(attended_low, grad_branch)
     attention_output_grad = contract_cols(grad_branch, w_out).astype(brain_float_cast)
-    heads_gradient = attention_output_grad.reshape(
-        token_rows, KEY_VALUE_HEADS, group_of_heads, HEAD_SIZE
-    )
-    correction = jnp.sum(
-        heads_gradient.astype(single_precision)
-        * attention_output.reshape(token_rows, KEY_VALUE_HEADS, group_of_heads, HEAD_SIZE),
-        axis=-1,
-    )
-    grad_query_heads = []
-    grad_key_heads = []
-    grad_value_heads = []
-    for key_value_head in range(KEY_VALUE_HEADS):
-        q_block = query_list[key_value_head]
-        log_total = log_totals[key_value_head]
-        grad_rows_head = heads_gradient[:, key_value_head].reshape(
-            token_rows * group_of_heads, HEAD_SIZE
-        )
-        row_delta = correction[:, key_value_head].reshape(token_rows * group_of_heads)
-        grad_query = jnp.zeros((token_rows * group_of_heads, HEAD_SIZE), single_precision)
-        key_parts = []
-        value_parts = []
-        for source in range(axis_parts):
-            scores = block_scores(q_block, key_value_head, source)
-            prob_block = jnp.where(allowed_list[source], jnp.exp(scores - log_total[:, None]), 0.0)
-            key_block = key_all[
-                source * token_rows : (source + 1) * token_rows,
-                key_value_head * HEAD_SIZE : (key_value_head + 1) * HEAD_SIZE,
-            ]
-            value_block = value_all[
-                source * token_rows : (source + 1) * token_rows,
-                key_value_head * HEAD_SIZE : (key_value_head + 1) * HEAD_SIZE,
-            ]
-            grad_prob = contract_cols(grad_rows_head, value_block)
-            grad_score = (prob_block * (grad_prob - row_delta[:, None])).astype(brain_float_cast)
-            grad_query = (
-                grad_query
-                + jnp.dot(grad_score, key_block, preferred_element_type=single_precision)
-                * score_scale
-            )
-            key_parts.append(contract_rows(grad_score, q_block) * score_scale)
-            value_parts.append(contract_rows(prob_block.astype(brain_float_cast), grad_rows_head))
-        grad_query_heads.append(grad_query.reshape(token_rows, group_of_heads, HEAD_SIZE))
-        grad_key_heads.append(jnp.concatenate(key_parts, axis=0))
-        grad_value_heads.append(jnp.concatenate(value_parts, axis=0))
-    grad_key_all = jnp.concatenate(grad_key_heads, axis=1)
-    grad_value_all = jnp.concatenate(grad_value_heads, axis=1)
+    attention_shape = jax.ShapeDtypeStruct(key_heads.shape, single_precision)
+    grad_query_all, grad_key_heads, grad_value_heads = attention_call(
+        attention_backward_kernel,
+        place,
+        [rotated_queries, attention_output_grad, attention_output, log_totals],
+        [cosine_lanes, sine_lanes, before[None, :], key_heads, value_heads],
+        [brain_float_cast],
+        [attention_shape, attention_shape],
+        3,
+    )
+    grad_key_all = grad_key_heads.swapaxes(0, 1).reshape(sequence, KEY_VALUE_HEADS * HEAD_SIZE)
+    grad_value_all = grad_value_heads.swapaxes(0, 1).reshape(
+        sequence, KEY_VALUE_HEADS * HEAD_SIZE
+    )
+    grad_key_all, grad_value_all, owned_ffn = lax.optimization_barrier(
+        (grad_key_all, grad_value_all, owned_ffn)
+    )
     key_value_gradient = lax.psum_scatter(
         jnp.concatenate([grad_key_all, grad_value_all], axis=1).astype(jnp.bfloat16),
         "mp",
@@ -327,15 +368,14 @@
     ).astype(jnp.float32)
     key_gradient = key_value_gradient[:, : KEY_VALUE_HEADS * HEAD_SIZE]
     grad_value = key_value_gradient[:, KEY_VALUE_HEADS * HEAD_SIZE :]
-    grad_query_all = jnp.stack(grad_query_heads, axis=1).reshape(token_rows, QUERY_HEADS, HEAD_SIZE)
-    grad_query_all = rotation_backward(grad_query_all, cosine_table, sine_lookup).reshape(
-        token_rows, QUERY_WIDTH
-    )
-    key_gradient = rotation_backward(
-        key_gradient.reshape(token_rows, KEY_VALUE_HEADS, HEAD_SIZE), cosine_table, sine_lookup
-    ).reshape(token_rows, KEY_VALUE_HEADS * HEAD_SIZE)
-    grad_qkv = jnp.concatenate([grad_query_all, key_gradient, grad_value], axis=1).astype(
-        brain_float_cast
+    key_gradient = key_gradient * cosine_lanes - swapped(key_gradient) * sine_lanes
+    grad_qkv = jnp.concatenate(
+        [
+            grad_query_all,
+            key_gradient.astype(brain_float_cast),
+            grad_value.astype(brain_float_cast),
+        ],
+        axis=1,
     )
     grad_bias = jnp.sum(grad_qkv.astype(single_precision), axis=0)
     grad_qkv_w = contract_rows(normed, grad_qkv)

time: 931 us -> 753 us (0.81)
  matrix products: 237 us -> 101 us
  local copies, waits for them, and re-layouts: 126 us -> 46.3 us
  waiting for transfers between devices: 398 us -> 445 us
  other arithmetic: 93.9 us -> 51.6 us
  Pallas kernels: 0 us -> 35.7 us
    dot_general x20 -> x4, matrix products: 83.9 us -> 30.2 us  [contract_cols(): lax.dot_general(left, right, (((1,), (1,)), ((), ())), preferred_element_...]
    dot_general x20 -> x4, matrix products: 73.7 us -> 29.4 us  [contract_rows(): lax.dot_general(left, right, (((0,), (0,)), ((), ())), preferred_element_...]
    dot_general x16 -> x0, matrix products: 38 us -> none  [the longest x8 25.8 us: per_device(): jnp.dot(prob_block, value_block, preferred_element_type=single_precision)]
    pallas_call x0 -> x2, Pallas kernels: none -> 35.7 us  [attention_call(): pl.pallas_call(kernel, grid_spec=pltpu.PrefetchScalarGridSpec(num_scalar_...]
    reshape x10 -> x1, local copies, waits for them, and re-layouts: 31.4 us -> 2.09 us  [per_device(): key_value_all.reshape(sequence, 2 * KEY_VALUE_HEADS, HEAD_SIZE)]
    reduce_sum x5 -> x0, other arithmetic: 26.1 us -> none  [the longest x4 25.8 us: per_device(): jnp.sum(shifted, axis=-1)]
    all_gather x1, waiting for transfers between devices: 0.01 us -> 21.2 us  [per_device(): lax.all_gather(out_weight.astype(brain_float_cast), 'dp', axis=0, tiled=T...]
    reduce_scatter x1, waiting for transfers between devices: 0.01 us -> 20.3 us  [per_device(): lax.psum_scatter(jnp.concatenate([grad_key_all, grad_value_all], axis=1)....]
  transfers between devices with their start and end apart: 12 -> 12, of which waited for: 8 -> 12; matrix products, arithmetic and copies ran while one was open for 28% -> 12% of each run, Pallas kernels for 0% -> 5%
where the time goes in v2:
time: 753 us; the launch traced here: 745 us
  waiting for transfers between devices  445 us (59%)
  matrix products  101 us (13%)
  other arithmetic  51.6 us (7%)
  blocking collectives  46.6 us (6%)
  local copies, waits for them, and re-layouts  46.3 us (6%)
  Pallas kernels  35.7 us (5%)
  between operations  17.7 us (2%)
    all_gather x1, waiting for transfers between devices, per_device(): lax.all_gather(jnp.concatenate([gate_up_weight[:, 0], gate_up_weight[:, 1...  106 us
    reduce_scatter x1, waiting for transfers between devices, per_device(): lax.psum_scatter(grad_ffn, 'dp', scatter_dimension=0, tiled=True)  96.1 us
    all_gather x1, waiting for transfers between devices, per_device(): lax.all_gather(jnp.concatenate([qkv_weight.astype(brain_float_cast), pack...  51.2 us
    psum x1, blocking collectives, per_device(): lax.psum(grad_vectors, ('dp', 'mp'))  39.6 us
    reduce_scatter x1, waiting for transfers between devices, per_device(): lax.psum_scatter(contract_cols(active, w_down_t).astype(jnp.bfloat16), 'm...  37.2 us
    pallas_call x2, Pallas kernels, attention_call(): pl.pallas_call(kernel, grid_spec=pltpu.PrefetchScalarGridSpec(num_scalar_...  35.7 us
    reduce_scatter x1, waiting for transfers between devices, per_device(): lax.psum_scatter(grad_attention, 'mp', scatter_dimension=1, tiled=True)  34.7 us
    all_gather x1, waiting for transfers between devices, per_device(): back_all = lax.all_gather(cotangent, 'mp', axis=0, tiled=True)  31.8 us
  transfers between devices with their start and end apart: 12, of which 12 were waited for; matrix products, arithmetic and copies ran while one was open for 12% of the time, Pallas kernels for 5%

profile of v2, /device:TPU:0, one launch (start us, length us, event | category | flops | bytes accessed | tf_op | source)
XLA Modules:
  0.0 745.2 jit_solution(10118245695300872272)
XLA Ops:
  14.4 51.2 %all-gather.7.cloned.1.call-done = bf16[896,1280]{1,0:T(8,128)(2,1)} async-done(((bf16[112,1280]{1,0:T(8,128)(2,1)}), bf16[896,1280]{1,0:T(8,128)(2,1)}) %all-gather.7.cloned.1.call-update) | async-done | bytes 2293776 | tf_op jit(solution)/shard_map/all_gather | solution.py:216
  78.9 8.9 %all-gather.9.cloned.1.call-done = bf16[2048,256]{1,0:T(8,128)(2,1)} async-done(((bf16[512,256]{1,0:T(8,128)(2,1)}), bf16[2048,256]{1,0:T(8,128)(2,1)}) %all-gather.9.cloned.1.call-update) | async-done | bytes 1048592 | tf_op jit(solution)/shard_map/all_gather | solution.py:272
  93.8 16.7 %shard_map.404 = (bf16[512,896]{1,0:T(8,128)(2,1)S(1)}, f32[512,896]{1,0:T(8,128)S(1)}, f32[512,896]{1,0:T(8,128)S(1)}) custom-call(s32[2]{0:T(128)S(1)} %pad_add_fusion.place, f32[512,1152]{1,0:T(8,128)S(1)} %copy-done.9, f32[512,128]{1,0:T(8,128)S(1)} %copy.122.cos_ref, f32[512,128]{1,0:T(8,128)S(1)} %copy.123.sin_ref, s32[512,1]{1,0:T(8,128)S(1)} %copy.124.start_ref, ...), custom_call_target="tpu_custom_call" | custom-call | flops 3758096384 | bytes 8388608 | tf_op jit(solution)/shard_map/pallas_call | solution.py:153
  113.6 21.2 %all-gather.15.cloned.1.call-done = bf16[896,896]{1,0:T(8,128)(2,1)} async-done(((bf16[112,896]{1,0:T(8,128)(2,1)}), bf16[896,896]{1,0:T(8,128)(2,1)}) %all-gather.15.cloned.1.call-update) | async-done | bytes 1605648 | tf_op jit(solution)/shard_map/all_gather | solution.py:231
  134.8 31.8 %all-gather.13.cloned.1.call-done = bf16[2048,896]{1,0:T(8,128)(2,1)} async-done(((bf16[512,896]{1,0:T(8,128)(2,1)}), bf16[2048,896]{1,0:T(8,128)(2,1)}) %all-gather.13.cloned.1.call-update) | async-done | bytes 3670032 | tf_op jit(solution)/shard_map/all_gather | solution.py:240
  166.6 106.1 %all-gather.11.cloned.1.call-done = bf16[896,3648]{1,0:T(8,128)(2,1)} async-done(((bf16[112,3648]{1,0:T(8,128)(2,1)}), bf16[896,3648]{1,0:T(8,128)(2,1)}) %all-gather.11.cloned.1.call-update) | async-done | bytes 6537232 | tf_op jit(solution)/shard_map/all_gather | solution.py:232
  278.4 29.5 %all-gather.17.cloned.1.call-done = bf16[2048,896]{1,0:T(8,128)(2,1)} async-done(((bf16[512,896]{1,0:T(8,128)(2,1)}), bf16[2048,896]{1,0:T(8,128)(2,1)}) %all-gather.17.cloned.1.call-update) | async-done | bytes 3670032 | tf_op jit(solution)/shard_map/all_gather | solution.py:297
  307.9 17.5 %fusion.3 = f32[2048,2432]{1,0:T(8,128)} fusion(bf16[2048,896]{1,0:T(8,128)(2,1)} %all-gather.17.cloned.1.call-done, bf16[896,3648]{1,0:T(8,128)(2,1)} %all-gather.11.cloned.1.call-done), kind=kOutput, calls=%fused_computation.11 | convolution fusion | flops 8925478912 | bytes 27951104 | tf_op jit(solution)/shard_map/dot_general | solution.py:300
  325.4 17.6 %multiply_convert_fusion.1 = (bf16[2048,1216]{1,0:T(8,128)(2,1)}, bf16[2048,1216]{1,0:T(8,128)(2,1)}, bf16[2048,1216]{1,0:T(8,128)(2,1)}) fusion(f32[2048,2432]{1,0:T(8,128)} %fusion.3, bf16[2048,896]{1,0:T(8,128)(2,1)} %all-gather.13.cloned.1.call-done, bf16[896,3648]{1,0:T(8,128)(2,1)} %all-gather.11.cloned.1.call-done), kind=kOutput, calls=%fused_computation.1 | convolution fusion | flops 4500094976 | bytes 41877504 | tf_op jit(solution)/shard_map/dot_general | solution.py:307
  343.0 7.5 %pad_maximum_fusion = bf16[2048,2432]{1,0:T(8,128)(2,1)S(1)} fusion(bf16[2048,1216]{1,0:T(8,128)(2,1)} %get-tuple-element.190, bf16[2048,1216]{1,0:T(8,128)(2,1)} %get-tuple-element.189), kind=kLoop, calls=%fused_computation.5 | loop fusion | flops 19922944 | bytes 19922944 | tf_op jit(solution)/shard_map/concatenate | solution.py:312
  350.5 3.8 copy-done.18
  354.4 14.7 %fusion.5 = bf16[2048,896]{1,0:T(8,128)(2,1)} fusion(bf16[2048,2432]{1,0:T(8,128)(2,1)S(1)} %pad_maximum_fusion, bf16[896,3648]{1,0:T(8,128)(2,1)} %all-gather.11.cloned.1.call-done), kind=kOutput, calls=%fused_computation.14 | convolution fusion | flops 8927313920 | bytes 17989632 | tf_op jit(solution)/shard_map/dot_general | solution.py:33
  369.1 9.5 %convolution_convert_fusion.3 = bf16[2048,896]{1,0:T(8,128)(2,1)} fusion(bf16[2048,1216]{1,0:T(8,128)(2,1)} %get-tuple-element.48, bf16[896,3648]{1,0:T(8,128)(2,1)} %all-gather.11.cloned.1.call-done), kind=kOutput, calls=%fused_computation.17 | convolution fusion | flops 4464574464 | bytes 11206656 | tf_op jit(solution)/shard_map/dot_general | solution.py:33
  379.1 10.4 %convolution_convert_fusion.2 = bf16[896,1216]{0,1:T(8,128)(2,1)} fusion(bf16[2048,896]{1,0:T(8,128)(2,1)} %all-gather.13.cloned.1.call-done, bf16[2048,1216]{1,0:T(8,128)(2,1)} %get-tuple-element.48), kind=kOutput, calls=%fused_computation.16 | convolution fusion | flops 4463828992 | bytes 10829824 | tf_op jit(solution)/shard_map/dot_general | solution.py:27
  392.7 13.7 %convolution_convert_fusion = bf16[896,2432]{1,0:T(8,128)(2,1)S(1)} fusion(bf16[2048,896]{1,0:T(8,128)(2,1)} %all-gather.17.cloned.1.call-done, bf16[2048,2432]{1,0:T(8,128)(2,1)} %copy-done.18), kind=kOutput, calls=%fused_computation.7 | convolution fusion | flops 8927657984 | bytes 17989632 | tf_op jit(solution)/shard_map/dot_general | solution.py:27
  417.3 37.2 %reduce-scatter.7.cloned.1.call-done = bf16[512,896]{1,0:T(8,128)(2,1)} async-done(((bf16[2048,896]{1,0:T(8,128)(2,1)}), bf16[512,896]{1,0:T(8,128)(2,1)}) %reduce-scatter.7.cloned.1.call-update) | async-done | bytes 917520 | tf_op jit(solution)/shard_map/reduce_scatter | solution.py:320
  461.0 19.0 %shard_map.405 = (bf16[512,896]{1,0:T(8,128)(2,1)S(1)}, f32[2,2048,64]{2,1,0:T(8,128)S(1)}, f32[2,2048,64]{2,1,0:T(8,128)S(1)}) custom-call(s32[2]{0:T(128)S(1)} %pad_add_fusion.place, bf16[512,896]{1,0:T(8,128)(2,1)S(1)} %copy-done.13, bf16[512,896]{1,0:T(8,128)(2,1)S(1)} %convolution_convert_fusion.5.do_ref, f32[512,896]{1,0:T(8,128)S(1)} %copy-done.2, ...), custom_call_target="tpu_custom_call" | custom-call | flops 11274289152 | bytes 8388608 | tf_op jit(solution)/shard_map/pallas_call | solution.py:153
  485.3 96.1 %reduce-scatter.11.cloned.1.call-done = bf16[112,3648]{1,0:T(8,128)(2,1)} async-done(((bf16[896,3648]{1,0:T(8,128)(2,1)}), bf16[112,3648]{1,0:T(8,128)(2,1)}) %reduce-scatter.11.cloned.1.call-update) | async-done | bytes 817168 | tf_op jit(solution)/shard_map/reduce_scatter | solution.py:335
  593.2 20.3 %reduce-scatter.13.cloned.1.call-done = bf16[512,256]{1,0:T(8,128)(2,1)} async-done(((bf16[2048,256]{1,0:T(8,128)(2,1)}), bf16[512,256]{1,0:T(8,128)(2,1)}) %reduce-scatter.13.cloned.1.call-update) | async-done | bytes 262160 | tf_op jit(solution)/shard_map/reduce_scatter | solution.py:363
  625.8 34.7 %reduce-scatter.15.cloned.1.call-done = bf16[896,512]{1,0:T(8,128)(2,1)} async-done(((bf16[896,2048]{1,0:T(8,128)(2,1)}), bf16[896,512]{1,0:T(8,128)(2,1)}) %reduce-scatter.15.cloned.1.call-update) | async-done | bytes 917520 | tf_op jit(solution)/shard_map/reduce_scatter | solution.py:390
  671.5 4.8 fusion.21
  676.5 39.6 %psum.7 = f32[8,368]{1,0:T(8,128)S(1)} all-reduce(f32[8,368]{1,0:T(8,128)S(1)} %pad_maximum_fusion.9), channel_id=1, replica_groups=mesh['dp'=8,'mp'=4] {'dp','mp'}, use_global_device_ids=true, to_apply=%region_14.15 | all-reduce | flops 2944 | bytes 23552 | tf_op jit(solution)/shard_map/psum | solution.py:406
  720.8 6.3 reduce-scatter.17.cloned.1.call-done
  727.1 7.0 all_gather.27
  (212 shorter events, 102.3 us)
Async XLA Ops:
  7.2 58.4 %all-gather.7.cloned.1.call-start = ((), (), s32[]{:S(2)}) async-start(), calls=%async_computation.6 | async-start | bytes 2580480 | tf_op jit(solution)/shard_map/all_gather | solution.py:216
  11.5 76.3 %all-gather.9.cloned.1.call-start = ((), (), s32[]{:S(2)}) async-start(), calls=%async_computation.7 | async-start | bytes 1310720 | tf_op jit(solution)/shard_map/all_gather | solution.py:272
  14.4 55.7 %copy-start.41 = (f32[512]{0:T(512)}, f32[512]{0:T(512)S(1)}, u32[]{:S(2)}) copy-start(f32[512]{0:T(512)S(1)} %add_rsqrt_fusion.1) | copy-start | bytes 6148
  72.4 62.5 %all-gather.15.cloned.1.call-start = ((), (), s32[]{:S(2)}) async-start(), calls=%async_computation.10 | async-start | bytes 1806336 | tf_op jit(solution)/shard_map/all_gather | solution.py:231
  73.1 93.5 %all-gather.13.cloned.1.call-start = ((), (), s32[]{:S(2)}) async-start(), calls=%async_computation.9 | async-start | bytes 4587520 | tf_op jit(solution)/shard_map/all_gather | solution.py:240
  73.7 199.0 %all-gather.11.cloned.1.call-start = ((), (), s32[]{:S(2)}) async-start(), calls=%async_computation.8 | async-start | bytes 7483392 | tf_op jit(solution)/shard_map/all_gather | solution.py:232
  75.4 232.5 %all-gather.17.cloned.1.call-start = ((), (), s32[]{:S(2)}) async-start(), calls=%async_computation.11 | async-start | bytes 4587520 | tf_op jit(solution)/shard_map/all_gather | solution.py:297
  113.6 162.1 %copy-start.1 = (f32[512,896]{1,0:T(8,128)}, f32[512,896]{1,0:T(8,128)S(1)}, u32[]{:S(2)}) copy-start(f32[512,896]{1,0:T(8,128)S(1)} %get-tuple-element.44.o_ref) | copy-start | bytes 5505028
  113.6 162.1 %copy-start.12 = (bf16[512,896]{1,0:T(8,128)(2,1)}, bf16[512,896]{1,0:T(8,128)(2,1)S(1)}, u32[]{:S(2)}) copy-start(bf16[512,896]{1,0:T(8,128)(2,1)S(1)} %get-tuple-element.51.q_ref) | copy-start | bytes 2752516
  278.1 132.4 %reduce-scatter.9.cloned.1.call-start = ((), (), s32[]{:S(2)}) async-start(), calls=%async_computation.13 | async-start | bytes 4587520 | tf_op jit(solution)/shard_map/reduce_scatter | solution.py:314
  369.1 85.4 %reduce-scatter.7.cloned.1.call-start = ((), (), s32[]{:S(2)}) async-start(), calls=%async_computation.12 | async-start | bytes 4587520 | tf_op jit(solution)/shard_map/reduce_scatter | solution.py:320
  378.7 202.7 %reduce-scatter.11.cloned.1.call-start = ((), (), s32[]{:S(2)}) async-start(), calls=%async_computation.14 | async-start | bytes 7483392 | tf_op jit(solution)/shard_map/reduce_scatter | solution.py:335
  413.1 41.3 %copy-start.28 = (bf16[512,896]{1,0:T(8,128)(2,1)S(1)}, bf16[512,896]{1,0:T(8,128)(2,1)}, u32[]{:S(2)}) copy-start(bf16[512,896]{1,0:T(8,128)(2,1)} %param.22) | copy-start | bytes 2752516
  413.2 200.3 %reduce-scatter.13.cloned.1.call-start = ((), (), s32[]{:S(2)}) async-start(), calls=%async_computation.15 | async-start | bytes 1310720 | tf_op jit(solution)/shard_map/reduce_scatter | solution.py:363
  485.3 98.5 %copy-start.32 = (bf16[2048,2,64]{0,2,1:T(8,128)(2,1)S(1)}, bf16[2048,2,64]{0,2,1:T(8,128)(2,1)}, u32[]{:S(2)}) copy-start(bf16[2048,2,64]{0,2,1:T(8,128)(2,1)} %copy.131) | copy-start | bytes 1572868
  589.3 71.2 %reduce-scatter.15.cloned.1.call-start = ((), (), s32[]{:S(2)}) async-start(), calls=%async_computation.16 | async-start | bytes 4587520 | tf_op jit(solution)/shard_map/reduce_scatter | solution.py:390
  619.1 108.0 %reduce-scatter.17.cloned.1.call-start = ((), (), s32[]{:S(2)}) async-start(), calls=%async_computation.17 | async-start | bytes 1032192 | tf_op jit(solution)/shard_map/reduce_scatter | solution.py:391
  671.4 44.8 %copy-start.43 = (f32[2,112]{1,0:T(2,128)S(1)}, f32[2,112]{1,0:T(2,128)}, u32[]{:S(2)}) copy-start(f32[2,112]{1,0:T(2,128)} %param.39) | copy-start | bytes 2692
  671.5 44.8 %copy-start.46 = (f32[2,112]{1,0:T(2,128)S(1)}, f32[2,112]{1,0:T(2,128)}, u32[]{:S(2)}) copy-start(f32[2,112]{1,0:T(2,128)} %param.41) | copy-start | bytes 2692
  671.5 44.8 %copy-start.47 = (f32[2,112]{1,0:T(2,128)S(1)}, f32[2,112]{1,0:T(2,128)}, u32[]{:S(2)}) copy-start(f32[2,112]{1,0:T(2,128)} %param.40) | copy-start | bytes 2692
  671.5 45.4 %copy-start.40 = (f32[144]{0:T(256)S(1)}, f32[144]{0:T(256)}, u32[]{:S(2)}) copy-start(f32[144]{0:T(256)} %param.27) | copy-start | bytes 1732
  671.5 45.4 %copy-start.48 = (f32[144]{0:T(256)S(1)}, f32[144]{0:T(256)}, u32[]{:S(2)}) copy-start(f32[144]{0:T(256)} %param.29) | copy-start | bytes 1732
  671.5 45.4 %copy-start.49 = (f32[144]{0:T(256)S(1)}, f32[144]{0:T(256)}, u32[]{:S(2)}) copy-start(f32[144]{0:T(256)} %param.28) | copy-start | bytes 1732
  671.5 46.0 %copy-start.15 = (f32[512,896]{1,0:T(8,128)S(1)}, f32[512,896]{1,0:T(8,128)}, u32[]{:S(2)}) copy-start(f32[512,896]{1,0:T(8,128)} %copy-done.14) | copy-start | bytes 5505028
  (39 other events, 150.6 us)
Sparse Core Ops, SparseCore 0:
  11.6 53.9 all-gather.6
  72.5 15.2 all-gather.8
  90.5 44.2 all-gather.14
  136.3 30.3 all-gather.12
  169.2 103.5 all-gather.10
  278.3 29.5 all-gather.16
  369.2 41.2 reduce-scatter.8
  413.2 41.2 reduce-scatter.6
  458.1 123.2 reduce-scatter.10
  589.4 23.9 reduce-scatter.12
  619.2 41.2 reduce-scatter.14
  664.1 63.0 reduce-scatter.16
